TPU v7x, 256 devices: a whole 4x4x8 slice. The times are simulated.
256 devices in a mesh: dev: 256 (over x, z, y, core).
Axes of the slice: x: 4, y: 4, z: 8, core: 2. Of those that a mesh axis runs over, the one named last changes fastest.
Arguments:
- embeddings: bfloat16 [262144, 768], P('dev')
Outputs:
- keep_weight: float32 [262144], P('dev')
All inputs are finite; a program needn't handle non-finite values.
Results may differ from a plain program's by a relative error of at most 0.0044.
Values may be sent and summed in bfloat16 or wider, within the bound.
No kernel may reach another device: no remote copies, remote signals or barrier semaphores. Data moves between devices by JAX's collectives and lax.ppermute only.
A program may use at most 64 MiB of HBM per device.

v0:
```python
import math

import jax
import jax.numpy as jnp
from jax import lax
from jax.sharding import PartitionSpec as P

ROUNDS = 4


sharpness = 10.0


def swapped(value, axis, stride):
    mask = 2**stride
    pairs = [(source, source ^ mask) for source in range(lax.axis_size(axis))]
    return lax.ppermute(value, axis, pairs)


def normalize(values):
    widened = values.astype(jnp.float32)
    scaled = (
        widened
        * lax.rsqrt(jnp.mean(widened * widened, axis=1, keepdims=True) + 1e-06)
        / math.sqrt(values.shape[1])
    )
    return scaled.astype(jnp.bfloat16)


def kernel_tile(left, right):
    similarity = lax.dot_general(
        left, right, (((1,), (1,)), ((), ())), preferred_element_type=jnp.float32
    )
    return jnp.exp(sharpness * (similarity - 1.0))


def fetch_partner(normed, bit_number):
    return swapped(normed, "dev", bit_number)


def shards(embeddings):
    normed = normalize(embeddings)
    player_count = lax.axis_size("dev")
    levels = player_count.bit_length() - 1
    tile_rows = normed.shape[0]
    bit_list = [levels - 1 - round_index for round_index in range(ROUNDS)]
    density = jnp.sum(kernel_tile(normed, normed), axis=1)
    for round_index in range(ROUNDS):
        bit_number = bit_list[round_index]
        partner = fetch_partner(normed, bit_number)
        density = density + jnp.sum(kernel_tile(normed, partner), axis=1)
    weights = 1.0 / density
    total = lax.psum(jnp.sum(weights), "dev")
    return weights * (player_count * tile_rows) / total


def solution(mesh):
    return jax.shard_map(
        shards,
        mesh=mesh,
        in_specs=(P("dev", None),),
        out_specs=P("dev"),
        check_vma=False,
    )
```

profile of v0, /device:TPU:1, one launch (start us, length us, event | category | flops | bytes accessed | tf_op | source)
XLA Modules:
  0.0 227.0 jit_solution(11128787972473955909)
XLA Ops:
  0.0 0.0 copy-start
  0.0 1.9 fusion
  1.9 0.0 copy-done
  1.9 0.4 fusion.2
  2.4 7.8 %collective-permute-start.2 = (bf16[1024,768]{1,0:T(8,128)(2,1)S(1)}, bf16[1024,768]{1,0:T(8,128)(2,1)S(1)}, u32[]{:S(2)}, u32[]{:S(2)}) collective-permute-start(bf16[1024,768]{1,0:T(8,128)(2,1)S(1)} %fusion.2), channel_id=1, source_target_pairs={{0,32},{1,33},{2,34},{3,35},{4,36},{5,37},{6,38},{7,39},{8,40},{9,... | collective-permute-start | bytes 4718600 | tf_op jit(solution)/shard_map/ppermute | solution.py:17
  10.2 1.2 collective-permute-start.1
  11.4 2.5 %collective-permute-start = (bf16[1024,768]{1,0:T(8,128)(2,1)S(1)}, bf16[1024,768]{1,0:T(8,128)(2,1)S(1)}, u32[]{:S(2)}, u32[]{:S(2)}) collective-permute-start(bf16[1024,768]{1,0:T(8,128)(2,1)S(1)} %fusion.2), channel_id=1, source_target_pairs={{0,128},{1,129},{2,130},{3,131},{4,132},{5,133},{6,134},{7,135},{8... | collective-permute-start | bytes 4718600 | tf_op jit(solution)/shard_map/ppermute | solution.py:17
  13.8 1.2 collective-permute-start.3
  15.0 1.9 exponential_reduce_fusion.4
  17.0 36.3 %collective-permute-done.2 = bf16[1024,768]{1,0:T(8,128)(2,1)S(1)} collective-permute-done((bf16[1024,768]{1,0:T(8,128)(2,1)S(1)}, bf16[1024,768]{1,0:T(8,128)(2,1)S(1)}, u32[]{:S(2)}, u32[]{:S(2)}) %collective-permute-start.2) | collective-permute-done | bytes 1572896 | tf_op jit(solution)/shard_map/ppermute | solution.py:17
  53.3 1.9 exponential_reduce_fusion.1
  55.3 0.0 collective-permute-done.1
  55.3 1.9 exponential_reduce_fusion.2
  57.2 23.8 %collective-permute-done = bf16[1024,768]{1,0:T(8,128)(2,1)S(1)} collective-permute-done((bf16[1024,768]{1,0:T(8,128)(2,1)S(1)}, bf16[1024,768]{1,0:T(8,128)(2,1)S(1)}, u32[]{:S(2)}, u32[]{:S(2)}) %collective-permute-start) | collective-permute-done | bytes 1572896 | tf_op jit(solution)/shard_map/ppermute | solution.py:17
  81.0 1.9 exponential_reduce_fusion.3
  83.0 64.0 %collective-permute-done.3 = bf16[1024,768]{1,0:T(8,128)(2,1)S(1)} collective-permute-done((bf16[1024,768]{1,0:T(8,128)(2,1)S(1)}, bf16[1024,768]{1,0:T(8,128)(2,1)S(1)}, u32[]{:S(2)}, u32[]{:S(2)}) %collective-permute-start.3) | collective-permute-done | bytes 1572896 | tf_op jit(solution)/shard_map/ppermute | solution.py:17
  147.0 1.9 exponential_reduce_fusion
  148.9 0.6 fusion.3
  149.5 76.2 %psum.7 = f32[]{:T(128)} all-reduce(f32[]{:T(128)} %get-tuple-element.5), channel_id=1, replica_groups=mesh['dev'=256] {'dev'}, use_global_device_ids=true, to_apply=%region_7.0 | all-reduce | flops 1 | bytes 8 | tf_op jit(solution)/shard_map/psum | solution.py:53
  225.7 1.3 multiply_divide_fusion
  (1 shorter events, 0.0 us)
Async XLA Ops:
  0.0 1.9 copy-start
  2.4 51.0 %collective-permute-start.2 = (bf16[1024,768]{1,0:T(8,128)(2,1)S(1)}, bf16[1024,768]{1,0:T(8,128)(2,1)S(1)}, u32[]{:S(2)}, u32[]{:S(2)}) collective-permute-start(bf16[1024,768]{1,0:T(8,128)(2,1)S(1)} %fusion.2), channel_id=1, source_target_pairs={{0,32},{1,33},{2,34},{3,35},{4,36},{5,37},{6,38},{7,39},{8,40},{9,... | collective-permute-start | bytes 4718600 | tf_op jit(solution)/shard_map/ppermute | solution.py:17
  10.2 45.1 %collective-permute-start.1 = (bf16[1024,768]{1,0:T(8,128)(2,1)S(1)}, bf16[1024,768]{1,0:T(8,128)(2,1)S(1)}, u32[]{:S(2)}, u32[]{:S(2)}) collective-permute-start(bf16[1024,768]{1,0:T(8,128)(2,1)S(1)} %fusion.2), channel_id=1, source_target_pairs={{0,64},{1,65},{2,66},{3,67},{4,68},{5,69},{6,70},{7,71},{8,72},{9,... | collective-permute-start | bytes 4718600 | tf_op jit(solution)/shard_map/ppermute | solution.py:17
  11.4 69.6 %collective-permute-start = (bf16[1024,768]{1,0:T(8,128)(2,1)S(1)}, bf16[1024,768]{1,0:T(8,128)(2,1)S(1)}, u32[]{:S(2)}, u32[]{:S(2)}) collective-permute-start(bf16[1024,768]{1,0:T(8,128)(2,1)S(1)} %fusion.2), channel_id=1, source_target_pairs={{0,128},{1,129},{2,130},{3,131},{4,132},{5,133},{6,134},{7,135},{8... | collective-permute-start | bytes 4718600 | tf_op jit(solution)/shard_map/ppermute | solution.py:17
  13.8 133.1 %collective-permute-start.3 = (bf16[1024,768]{1,0:T(8,128)(2,1)S(1)}, bf16[1024,768]{1,0:T(8,128)(2,1)S(1)}, u32[]{:S(2)}, u32[]{:S(2)}) collective-permute-start(bf16[1024,768]{1,0:T(8,128)(2,1)S(1)} %fusion.2), channel_id=1, source_target_pairs={{0,16},{1,17},{2,18},{3,19},{4,20},{5,21},{6,22},{7,23},{8,24},{9,... | collective-permute-start | bytes 4718600 | tf_op jit(solution)/shard_map/ppermute | solution.py:17
where the time goes:
time: 227 us
  waiting for transfers between devices  124 us (55%)
  blocking collectives  76.2 us (34%)
  starting transfers between devices  12.7 us (6%)
  matrix products  9.62 us (4%)
  other arithmetic  4.23 us (2%)
    ppermute x4, waiting for transfers between devices, swapped(): return lax.ppermute(value, axis, pairs)  124 us
    psum x1, blocking collectives, shards(): total = lax.psum(jnp.sum(weights), 'dev')  76.2 us
    ppermute x4, starting transfers between devices, swapped(): return lax.ppermute(value, axis, pairs)  12.7 us
    dot_general x5, matrix products, kernel_tile(): lax.dot_general(left, right, (((1,), (1,)), ((), ())), preferred_element_...  9.62 us
  transfers between devices with their start and end apart: 4, of which 3 were waited for; matrix products, arithmetic and copies ran while one was open for 3% of the time, Pallas kernels for 0%

commit v1 on v0

v1 whole, which is shorter than its diff:
```python
import math

import jax
import jax.numpy as jnp
import numpy as np
from jax import lax
from jax.sharding import PartitionSpec as P

ROUNDS = 4


sharpness = 10.0


def parity(value):
    return bin(value).count("1") & 1


def plan(players):
    low = players.bit_length() - 1 - ROUNDS
    z_near, z_swap = 1 << low, 3 << low
    x_near, x_swap = 4 << low, 12 << low
    first, second = [], []
    for player in range(players):
        if parity(player >> low) ^ (player & 1):
            first.append((player, player ^ x_near))
            second.append((player, player ^ z_swap))
        else:
            first.append((player, player ^ z_near))
            second.append((player, player ^ x_swap))
    return first, second


def inverse(pairs):
    return [(target, source) for source, target in pairs]


def normalize(values):
    widened = values.astype(jnp.float32)
    scaled = (
        widened
        * lax.rsqrt(jnp.mean(widened * widened, axis=1, keepdims=True) + 1e-06)
        / math.sqrt(values.shape[1])
    )
    return scaled.astype(jnp.bfloat16)


def kernel_tile(left, right):
    similarity = lax.dot_general(
        left, right, (((1,), (1,)), ((), ())), preferred_element_type=jnp.float32
    )
    return jnp.exp(sharpness * (similarity - 1.0))


def shards(embeddings):
    players = lax.axis_size("dev")
    rows = embeddings.shape[0]
    first, second = plan(players)
    near = lax.ppermute(embeddings, "dev", first)
    far = lax.ppermute(embeddings, "dev", second)
    own = normalize(embeddings)
    near = normalize(near)
    far = normalize(far)
    density = jnp.sum(kernel_tile(own, own), axis=1)
    own_near = kernel_tile(own, near)
    near_far = kernel_tile(near, far)
    to_near = jnp.sum(own_near, axis=0) + jnp.sum(near_far, axis=1)
    to_far = jnp.sum(near_far, axis=0)
    density = density + jnp.sum(own_near, axis=1)
    density = density + lax.ppermute(to_near, "dev", inverse(first))
    density = density + lax.ppermute(to_far, "dev", inverse(second))
    weights = 1.0 / density
    totals = lax.all_to_all(
        jnp.full((players, 128), jnp.sum(weights)), "dev", 0, 0, tiled=True
    )
    total = jnp.sum(totals[:, 0])
    return weights * (players * rows) / total


def solution(mesh):
    return jax.shard_map(
        shards,
        mesh=mesh,
        in_specs=(P("dev", None),),
        out_specs=P("dev"),
        check_vma=False,
    )
```

time: 227 us -> 82.5 us (0.36)
  waiting for transfers between devices: 124 us -> 32.3 us
  blocking collectives: 76.2 us -> 25.4 us
  matrix products: 9.62 us -> 6.48 us
    ppermute x4, waiting for transfers between devices: 124 us -> 32.3 us  [the longest x1 29 us: shards(): near = lax.ppermute(embeddings, 'dev', first)]
    psum x1 -> x0, blocking collectives: 76.2 us -> none  [shards(): total = lax.psum(jnp.sum(weights), 'dev')]
    all_to_all x0 -> x1, blocking collectives: none -> 25.4 us  [shards(): lax.all_to_all(jnp.full((players, 128), jnp.sum(weights)), 'dev', 0, 0, t...]
    dot_general x5 -> x3, matrix products: 9.62 us -> 6.48 us  [kernel_tile(): lax.dot_general(left, right, (((1,), (1,)), ((), ())), preferred_element_...]
  transfers between devices with their start and end apart: 4 -> 4, of which waited for: 3 -> 2; matrix products, arithmetic and copies ran while one was open for 3% -> 5% of each run, Pallas kernels for 0% -> 0%
where the time goes in v1:
time: 82.5 us; the launch traced here: 82.3 us
  waiting for transfers between devices  32.3 us (39%)
  blocking collectives  25.4 us (31%)
  starting transfers between devices  12.1 us (15%)
  matrix products  6.48 us (8%)
  other arithmetic  5.2 us (6%)
    ppermute x1, waiting for transfers between devices, shards(): near = lax.ppermute(embeddings, 'dev', first)  29 us
    all_to_all x1, blocking collectives, shards(): lax.all_to_all(jnp.full((players, 128), jnp.sum(weights)), 'dev', 0, 0, t...  25.4 us
    dot_general x3, matrix products, kernel_tile(): lax.dot_general(left, right, (((1,), (1,)), ((), ())), preferred_element_...  6.48 us
    ppermute x1, starting transfers between devices, shards(): far = lax.ppermute(embeddings, 'dev', second)  6.02 us
    ppermute x1, starting transfers between devices, shards(): density = density + lax.ppermute(to_far, 'dev', inverse(second))  3.97 us
    ppermute x1, waiting for transfers between devices, shards(): far = lax.ppermute(embeddings, 'dev', second)  3.33 us
    reduce_sum x3, other arithmetic, normalize(): jnp.mean(widened * widened, axis=1, keepdims=True) + 1e-06  2.56 us
    ppermute x1, starting transfers between devices, shards(): near = lax.ppermute(embeddings, 'dev', first)  2.04 us
  transfers between devices with their start and end apart: 4, of which 2 were waited for; matrix products, arithmetic and copies ran while one was open for 5% of the time, Pallas kernels for 0%

profile of v1, /device:TPU:1, one launch (start us, length us, event | category | flops | bytes accessed | tf_op | source)
XLA Modules:
  0.0 82.3 jit_solution(6358596069516555467)
XLA Ops:
  0.0 2.0 %collective-permute-start = (bf16[1024,768]{1,0:T(8,128)(2,1)}, bf16[1024,768]{1,0:T(8,128)(2,1)S(1)}, u32[]{:S(2)}, u32[]{:S(2)}) collective-permute-start(bf16[1024,768]{1,0:T(8,128)(2,1)} %param.1), channel_id=1, source_target_pairs={{0,16},{1,65},{2,18},{3,67},{4,20},{5,69},{6,22},{7,71},{8,24},{9,... | collective-permute-start | bytes 4718600 | tf_op jit(solution)/shard_map/ppermute | solution.py:59
  2.0 6.0 %collective-permute-start.1 = (bf16[1024,768]{1,0:T(8,128)(2,1)}, bf16[1024,768]{1,0:T(8,128)(2,1)S(1)}, u32[]{:S(2)}, u32[]{:S(2)}) collective-permute-start(bf16[1024,768]{1,0:T(8,128)(2,1)} %param.1), channel_id=1, source_target_pairs={{0,192},{1,49},{2,194},{3,51},{4,196},{5,53},{6,198},{7,55},{8,200... | collective-permute-start | bytes 4718600 | tf_op jit(solution)/shard_map/ppermute | solution.py:60
  8.1 1.8 %fusion.4 = f32[1024]{0:T(1024)S(1)} fusion(bf16[1024,768]{1,0:T(8,128)(2,1)} %param.1), kind=kLoop, calls=%fused_computation.13 | loop fusion | flops 2358272 | bytes 1576960 | tf_op jit(solution)/shard_map/reduce_sum | solution.py:42
  9.9 29.0 %collective-permute-done = bf16[1024,768]{1,0:T(8,128)(2,1)S(1)} collective-permute-done((bf16[1024,768]{1,0:T(8,128)(2,1)}, bf16[1024,768]{1,0:T(8,128)(2,1)S(1)}, u32[]{:S(2)}, u32[]{:S(2)}) %collective-permute-start) | collective-permute-done | bytes 1572896 | tf_op jit(solution)/shard_map/ppermute | solution.py:59
  38.9 0.4 fusion.7
  39.3 3.3 %collective-permute-done.1 = bf16[1024,768]{1,0:T(8,128)(2,1)S(1)} collective-permute-done((bf16[1024,768]{1,0:T(8,128)(2,1)}, bf16[1024,768]{1,0:T(8,128)(2,1)S(1)}, u32[]{:S(2)}, u32[]{:S(2)}) %collective-permute-start.1) | collective-permute-done | bytes 1572896 | tf_op jit(solution)/shard_map/ppermute | solution.py:60
  42.6 0.4 fusion.10
  43.0 0.0 copy-start
  43.0 2.2 %fusion.3 = (f32[1024]{0:T(1024)S(1)}, f32[1024]{0:T(1024)S(1)}) fusion(bf16[1024,768]{1,0:T(8,128)(2,1)S(1)} %collective-permute-done.1, f32[1024]{0:T(1024)S(1)} %add_rsqrt_fusion, bf16[1024,768]{1,0:T(8,128)(2,1)S(1)} %collective-permute-done, f32[1024]{0:T(1024)S(1)} %add_rsqrt_fusion.1), kind=kOutput, calls=%fused_computation.12 | convolution fusion | flops 1621096448 | bytes 3162112 | tf_op jit(solution)/shard_map/dot_general | solution.py:49
  45.2 0.0 copy-done
  45.3 2.2 %fusion.1 = (f32[1024]{0:T(1024)S(1)}, f32[1024]{0:T(1024)S(1)}) fusion(bf16[1024,768]{1,0:T(8,128)(2,1)S(1)} %collective-permute-done, f32[1024]{0:T(1024)S(1)} %add_rsqrt_fusion.1, bf16[1024,768]{1,0:T(8,128)(2,1)S(1)} %copy-done, f32[1024]{0:T(1024)S(1)} %add_rsqrt_fusion.2), kind=kOutput, calls=%fused_computation.10 | convolution fusion | flops 1621096448 | bytes 3162112 | tf_op jit(solution)/shard_map/dot_general | solution.py:49
  47.5 0.1 collective-permute-start.2
  47.6 4.0 %collective-permute-start.3 = (f32[1024]{0:T(1024)S(1)}, f32[1024]{0:T(1024)S(1)}, u32[]{:S(2)}, u32[]{:S(2)}) collective-permute-start(f32[1024]{0:T(1024)S(1)} %get-tuple-element.8), channel_id=1, source_target_pairs={{192,0},{49,1},{194,2},{51,3},{196,4},{53,5},{198,6},{55,7},{200,8... | collective-permute-start | bytes 12296 | tf_op jit(solution)/shard_map/ppermute | solution.py:71
  51.5 2.0 %exponential_reduce_fusion = f32[1024]{0:T(1024)S(1)} fusion(bf16[1024,768]{1,0:T(8,128)(2,1)S(1)} %copy-done, f32[1024]{0:T(1024)S(1)} %add_rsqrt_fusion.2), kind=kOutput, calls=%fused_computation.2 | convolution fusion | flops 1616903168 | bytes 1581056 | tf_op jit(solution)/shard_map/dot_general | solution.py:49
  53.6 0.0 collective-permute-done.2
  53.6 0.0 collective-permute-done.3
  53.6 0.6 fusion.25
  54.2 0.7 broadcast_in_dim.2
  55.0 25.4 %all_to_all.9 = f32[256,1,128]{2,1,0:T(1,128)S(1)} all-to-all(f32[256,1,128]{2,1,0:T(1,128)S(1)} %broadcast_in_dim.2), channel_id=1, replica_groups=mesh['dev'=256] {'dev'}, dimensions={0} | all-to-all | bytes 262144 | tf_op jit(solution)/shard_map/all_to_all | solution.py:73
  80.3 0.7 slice_reduce_fusion
  81.0 1.3 %multiply_divide_fusion = f32[1024]{0:T(1024)} fusion(f32[1024]{0:T(1024)S(1)} %get-tuple-element.10, f32[]{:T(128)} %slice_reduce_fusion), kind=kLoop, calls=%fused_computation.27 | loop fusion | flops 2048 | bytes 8196 | tf_op jit(solution)/shard_map/div | solution.py:77
  (4 shorter events, 0.0 us)
Async XLA Ops:
  0.0 38.9 %collective-permute-start = (bf16[1024,768]{1,0:T(8,128)(2,1)}, bf16[1024,768]{1,0:T(8,128)(2,1)S(1)}, u32[]{:S(2)}, u32[]{:S(2)}) collective-permute-start(bf16[1024,768]{1,0:T(8,128)(2,1)} %param.1), channel_id=1, source_target_pairs={{0,16},{1,65},{2,18},{3,67},{4,20},{5,69},{6,22},{7,71},{8,24},{9,... | collective-permute-start | bytes 4718600 | tf_op jit(solution)/shard_map/ppermute | solution.py:59
  2.0 40.6 %collective-permute-start.1 = (bf16[1024,768]{1,0:T(8,128)(2,1)}, bf16[1024,768]{1,0:T(8,128)(2,1)S(1)}, u32[]{:S(2)}, u32[]{:S(2)}) collective-permute-start(bf16[1024,768]{1,0:T(8,128)(2,1)} %param.1), channel_id=1, source_target_pairs={{0,192},{1,49},{2,194},{3,51},{4,196},{5,53},{6,198},{7,55},{8,200... | collective-permute-start | bytes 4718600 | tf_op jit(solution)/shard_map/ppermute | solution.py:60
  43.0 2.2 %copy-start = (bf16[1024,768]{1,0:T(8,128)(2,1)S(1)}, bf16[1024,768]{1,0:T(8,128)(2,1)}, u32[]{:S(2)}) copy-start(bf16[1024,768]{1,0:T(8,128)(2,1)} %param.1) | copy-start | bytes 4718596
  47.5 6.1 %collective-permute-start.2 = (f32[1024]{0:T(1024)S(1)}, f32[1024]{0:T(1024)S(1)}, u32[]{:S(2)}, u32[]{:S(2)}) collective-permute-start(f32[1024]{0:T(1024)S(1)} %add.43), channel_id=1, source_target_pairs={{16,0},{65,1},{18,2},{67,3},{20,4},{69,5},{22,6},{71,7},{24,8},{73... | collective-permute-start | bytes 12296 | tf_op jit(solution)/shard_map/ppermute | solution.py:70
  47.6 6.0 %collective-permute-start.3 = (f32[1024]{0:T(1024)S(1)}, f32[1024]{0:T(1024)S(1)}, u32[]{:S(2)}, u32[]{:S(2)}) collective-permute-start(f32[1024]{0:T(1024)S(1)} %get-tuple-element.8), channel_id=1, source_target_pairs={{192,0},{49,1},{194,2},{51,3},{196,4},{53,5},{198,6},{55,7},{200,8... | collective-permute-start | bytes 12296 | tf_op jit(solution)/shard_map/ppermute | solution.py:71

commit v2 on v1

v2 whole, which is shorter than its diff:
```python
import functools
import math

import jax
import jax.numpy as jnp
from jax import lax
from jax.experimental import pallas as pl
from jax.experimental.pallas import tpu as pltpu
from jax.sharding import PartitionSpec as P

ROUNDS = 4
LANES = 128
STEP = 256
LATE = 768

sharpness = 10.0
RATE = sharpness * math.log2(math.e)


def parity(value):
    return bin(value).count("1") & 1


def plan(players):
    low = players.bit_length() - 1 - ROUNDS
    z_near, z_swap = 1 << low, 3 << low
    x_near, x_swap = 4 << low, 12 << low
    near, far = ([], []), ([], [])
    for player in range(players):
        odd = (player >> (low - 1)) & 1
        if parity(player >> low) ^ (player & 1):
            near[1 - odd].append((player, player ^ x_near))
            far[odd].append((player, player ^ z_swap))
        else:
            near[odd].append((player, player ^ z_near))
            far[1 - odd].append((player, player ^ x_swap))
    return near, far


def inverse(pairs):
    return [(target, source) for source, target in pairs]


def is_late():
    me = lax.axis_index("dev")
    bits = me ^ (me >> 3) ^ (me >> 4) ^ (me >> 5) ^ (me >> 6) ^ (me >> 7)
    return lax.rem(bits, 2) == 0


def unit(values):
    widened = values.astype(jnp.float32)
    mean = jnp.mean(widened * widened, axis=1, keepdims=True)
    scale = lax.rsqrt(mean + 1e-06) * (1.0 / math.sqrt(values.shape[1]))
    return (widened * scale).astype(jnp.bfloat16)


def unit_rows(source, target):
    rows = source.shape[0]
    for start in range(0, rows, STEP):
        part = pl.ds(start, min(STEP, rows - start))
        target[part, :] = unit(source[part, :])


def put(target, start, vector, add):
    for k in range(vector.shape[1] // LANES):
        at = pl.ds(start // LANES + k, 1)
        part = vector[:, k * LANES : (k + 1) * LANES]
        target[at, :] = target[at, :] + part if add else part


def tile_sums(left, right, row_out, row_start, row_add, col_out, col_start, col_add):
    rows, cols = left.shape[0], right.shape[0]
    total = None
    for start in range(0, rows, STEP):
        similarity = lax.dot_general(
            left[pl.ds(start, STEP), :],
            right[...],
            (((1,), (1,)), ((), ())),
            preferred_element_type=jnp.float32,
        )
        value = jnp.exp2(similarity * RATE - RATE)
        folded = value[:, :LANES]
        for k in range(1, cols // LANES):
            folded = folded + value[:, k * LANES : (k + 1) * LANES]
        sums = jnp.sum(folded.T, axis=0, keepdims=True)
        put(row_out, row_start + start, sums, row_add)
        if col_out is not None:
            part = jnp.sum(value.reshape(STEP // 8, 8, cols), axis=0)
            total = part if total is None else total + part
    if col_out is not None:
        put(col_out, col_start, jnp.sum(total, axis=0, keepdims=True), col_add)


def own_kernel(raw, normed, first, second, density):
    unit_rows(raw, normed)
    first[...] = raw[pl.ds(0, LATE), :]
    second[...] = raw[pl.ds(LATE, raw.shape[0] - LATE), :]
    tile_sums(normed, normed, density, 0, False, None, 0, False)


def early_kernel(normed, near_raw, far_raw, density, density_out, to_near, to_far, near, far):
    density_out[...] = density[...]

    @pl.when(jnp.logical_not(is_late()))
    def _():
        unit_rows(near_raw, near)
        unit_rows(far_raw, far)
        tile_sums(normed, near, density_out, 0, True, to_near, 0, False)
        tile_sums(near, far, to_near, 0, True, to_far, 0, False)


def late_first_kernel(
    normed, near_raw, far_raw, density, to_near, to_far,
    density_out, near_out, far_out, near, far,
):
    density_out[...] = density[...]
    near_out[...] = to_near[...]
    far_out[...] = to_far[...]

    @pl.when(is_late())
    def _():
        unit_rows(near_raw, near)
        unit_rows(far_raw, far)
        tile_sums(normed, near, density_out, 0, True, near_out, 0, False)
        tile_sums(near, far, near_out, 0, True, far_out, 0, False)


def late_second_kernel(
    normed, near_first, far_first, near_raw, far_raw, density, to_near, to_far,
    density_out, near_out, far_out, near, far,
):
    density_out[...] = density[...]
    near_out[...] = to_near[...]
    far_out[...] = to_far[...]

    @pl.when(is_late())
    def _():
        unit_rows(near_raw, near)
        unit_rows(far_raw, far)
        tile_sums(normed, near, density_out, 0, True, near_out, LATE, False)
        tile_sums(near_first, far, near_out, 0, True, far_out, LATE, False)
        tile_sums(near, far_first, near_out, LATE, True, far_out, 0, True)
        tile_sums(near, far, near_out, LATE, True, far_out, LATE, True)


def weight_kernel(density, from_near, from_far, weights, total):
    value = 1.0 / (density[...] + from_near[...] + from_far[...])
    weights[...] = value
    total[...] = jnp.full(total.shape, jnp.sum(value))


def scale_kernel(weights, totals, keep, *, rows):
    total = jnp.sum(totals[...], axis=0, keepdims=True)
    keep[...] = weights[...] * rows / total


def call(kernel, operands, outs, scratch=(), flops=0):
    space = pl.BlockSpec(memory_space=pltpu.VMEM)
    shapes = [jax.ShapeDtypeStruct(*out) for out in outs]
    moved = sum(math.prod(s.shape) * s.dtype.itemsize for s in [*operands, *shapes])
    return pl.pallas_call(
        kernel,
        out_shape=shapes,
        in_specs=[space] * len(operands),
        out_specs=[space] * len(shapes),
        scratch_shapes=[pltpu.VMEM(*s) for s in scratch],
        cost_estimate=pl.CostEstimate(
            flops=flops, bytes_accessed=moved, transcendentals=0
        ),
        compiler_params=pltpu.CompilerParams(vmem_limit_bytes=32 * 2**20),
    )(*operands)


def shards(embeddings):
    players = lax.axis_size("dev")
    rows, width = embeddings.shape
    rest = rows - LATE
    bf16, f32 = jnp.bfloat16, jnp.float32
    sums = ((rows // LANES, LANES), f32)
    tile = 2 * rows * rows * width
    near, far = plan(players)

    near_early = lax.ppermute(embeddings, "dev", near[0])
    far_early = lax.ppermute(embeddings, "dev", far[0])
    normed, first, second, density = call(
        own_kernel,
        [embeddings],
        [((rows, width), bf16), ((LATE, width), bf16), ((rest, width), bf16), sums],
        flops=tile,
    )
    near_first = lax.ppermute(first, "dev", near[1])
    far_first = lax.ppermute(first, "dev", far[1])
    near_second = lax.ppermute(second, "dev", near[1])
    far_second = lax.ppermute(second, "dev", far[1])

    density, to_near, to_far = call(
        early_kernel,
        [normed, near_early, far_early, density],
        [sums, sums, sums],
        [((rows, width), bf16)] * 2,
        flops=2 * tile,
    )
    density, to_near, to_far, near_first, far_first = call(
        late_first_kernel,
        [normed, near_first, far_first, density, to_near, to_far],
        [sums, sums, sums] + [((LATE, width), bf16)] * 2,
        flops=tile * 21 // 16,
    )
    density, to_near, to_far = call(
        late_second_kernel,
        [normed, near_first, far_first, near_second, far_second, density, to_near, to_far],
        [sums, sums, sums],
        [((rest, width), bf16)] * 2,
        flops=tile * 11 // 16,
    )
    from_near = lax.ppermute(to_near, "dev", inverse(near[0] + near[1]))
    from_far = lax.ppermute(to_far, "dev", inverse(far[0] + far[1]))
    weights, total = call(
        weight_kernel, [density, from_near, from_far], [sums, ((players, LANES), f32)]
    )
    totals = lax.all_to_all(total, "dev", 0, 0, tiled=True)
    (keep,) = call(
        functools.partial(scale_kernel, rows=float(players * rows)), [weights, totals], [sums]
    )
    return keep.reshape(rows)


def solution(mesh):
    return jax.shard_map(
        shards,
        mesh=mesh,
        in_specs=(P("dev", None),),
        out_specs=P("dev"),
        check_vma=False,
    )
```

time: 82.5 us -> 87.2 us (1.057)
  Pallas kernels: 0 us -> 7.37 us
  blocking collectives: 25.4 us -> 32.2 us
  starting transfers between devices: 12.1 us -> 18.9 us
  matrix products: 6.48 us -> 0 us
  waiting for transfers between devices: 32.3 us -> 27 us
  other arithmetic: 5.2 us -> 0 us
    pallas_call x0 -> x6, Pallas kernels: none -> 7.37 us  [call(): pl.pallas_call(kernel, out_shape=shapes, in_specs=[space] * len(operands)...]
    all_to_all x1, blocking collectives: 25.4 us -> 32.2 us  [shards(): totals = lax.all_to_all(total, 'dev', 0, 0, tiled=True)]
    ppermute x4 -> x8, starting transfers between devices: 12.1 us -> 18.9 us  [the longest x1 8.76 us: shards(): far_early = lax.ppermute(embeddings, 'dev', far[0])]
    dot_general x3 -> x0, matrix products: 6.48 us -> none  [kernel_tile(): lax.dot_general(left, right, (((1,), (1,)), ((), ())), preferred_element_...]
    ppermute x4 -> x8, waiting for transfers between devices: 32.3 us -> 27 us  [the longest x1 20.3 us: shards(): far_early = lax.ppermute(embeddings, 'dev', far[0])]
    reduce_sum x5 -> x0, other arithmetic: 3.88 us -> none  [the longest x3 2.56 us: normalize(): jnp.mean(widened * widened, axis=1, keepdims=True) + 1e-06]
    unnamed x2, local copies, waits for them, and re-layouts: 0.01 us -> 1.41 us
    div x1 -> x0, other arithmetic: 1.29 us -> none  [shards(): return weights * (players * rows) / total]
  transfers between devices with their start and end apart: 4 -> 8, of which waited for: 2 -> 3; matrix products, arithmetic and copies ran while one was open for 5% -> 0% of each run, Pallas kernels for 0% -> 8%
where the time goes in v2:
time: 87.2 us; the launch traced here: 86.9 us
  blocking collectives  32.2 us (37%)
  waiting for transfers between devices  27 us (31%)
  starting transfers between devices  18.9 us (22%)
  Pallas kernels  7.37 us (8%)
  local copies, waits for them, and re-layouts  1.41 us (2%)
    all_to_all x1, blocking collectives, shards(): totals = lax.all_to_all(total, 'dev', 0, 0, tiled=True)  32.2 us
    ppermute x1, waiting for transfers between devices, shards(): far_early = lax.ppermute(embeddings, 'dev', far[0])  20.3 us
    ppermute x1, starting transfers between devices, shards(): far_early = lax.ppermute(embeddings, 'dev', far[0])  8.76 us
    pallas_call x6, Pallas kernels, call(): pl.pallas_call(kernel, out_shape=shapes, in_specs=[space] * len(operands)...  7.37 us
    ppermute x1, waiting for transfers between devices, shards(): near_early = lax.ppermute(embeddings, 'dev', near[0])  5.67 us
    ppermute x1, starting transfers between devices, shards(): from_far = lax.ppermute(to_far, 'dev', inverse(far[0] + far[1]))  4 us
    ppermute x1, starting transfers between devices, shards(): near_second = lax.ppermute(second, 'dev', near[1])  1.98 us
  transfers between devices with their start and end apart: 8, of which 3 were waited for; matrix products, arithmetic and copies ran while one was open for 0% of the time, Pallas kernels for 8%

profile of v2, /device:TPU:1, one launch (start us, length us, event | category | flops | bytes accessed | tf_op | source)
XLA Modules:
  0.0 86.9 jit_solution(8376103624359418351)
XLA Ops:
  0.0 1.3 %collective-permute-start.2 = (bf16[1024,768]{1,0:T(8,128)(2,1)}, bf16[1024,768]{1,0:T(8,128)(2,1)S(1)}, u32[]{:S(2)}, u32[]{:S(2)}) collective-permute-start(bf16[1024,768]{1,0:T(8,128)(2,1)} %raw.1), channel_id=1, source_target_pairs={{0,16},{2,18},{4,20},{6,22},{9,73},{11,75},{13,77},{15,79},{17,1},... | collective-permute-start | bytes 4718600 | tf_op jit(solution)/shard_map/ppermute | solution.py:183
  1.3 8.8 %collective-permute-start.3 = (bf16[1024,768]{1,0:T(8,128)(2,1)}, bf16[1024,768]{1,0:T(8,128)(2,1)S(1)}, u32[]{:S(2)}, u32[]{:S(2)}) collective-permute-start(bf16[1024,768]{1,0:T(8,128)(2,1)} %raw.1), channel_id=1, source_target_pairs={{1,49},{3,51},{5,53},{7,55},{8,200},{10,202},{12,204},{14,206},{16... | collective-permute-start | bytes 4718600 | tf_op jit(solution)/shard_map/ppermute | solution.py:184
  10.1 0.0 copy-start
  10.1 1.4 %copy-done = bf16[1024,768]{1,0:T(8,128)(2,1)S(1)} copy-done((bf16[1024,768]{1,0:T(8,128)(2,1)S(1)}, bf16[1024,768]{1,0:T(8,128)(2,1)}, u32[]{:S(2)}) %copy-start) | copy-done | bytes 1572888
  11.5 2.3 %shard_map.17 = (bf16[1024,768]{1,0:T(8,128)(2,1)S(1)}, bf16[768,768]{1,0:T(8,128)(2,1)S(1)}, bf16[256,768]{1,0:T(8,128)(2,1)S(1)}, f32[8,128]{1,0:T(8,128)S(1)}) custom-call(bf16[1024,768]{1,0:T(8,128)(2,1)S(1)} %copy-done), custom_call_target="tpu_custom_call" | custom-call | flops 1610612736 | bytes 4722688 | tf_op jit(solution)/shard_map/pallas_call | solution.py:161
  13.8 1.4 %collective-permute-start = (bf16[768,768]{1,0:T(8,128)(2,1)S(1)}, bf16[768,768]{1,0:T(8,128)(2,1)S(1)}, u32[]{:S(2)}, u32[]{:S(2)}) collective-permute-start(bf16[768,768]{1,0:T(8,128)(2,1)S(1)} %get-tuple-element.23), channel_id=1, source_target_pairs={{1,65},{3,67},{5,69},{7,71},{8,24},{10,26},{12,28},{14,30},{16,80}... | collective-permute-start | bytes 3538952 | tf_op jit(solution)/shard_map/ppermute | solution.py:191
  15.2 0.7 collective-permute-start.1
  15.9 2.0 %collective-permute-start.4 = (bf16[256,768]{1,0:T(8,128)(2,1)S(1)}, bf16[256,768]{1,0:T(8,128)(2,1)S(1)}, u32[]{:S(2)}, u32[]{:S(2)}) collective-permute-start(bf16[256,768]{1,0:T(8,128)(2,1)S(1)} %get-tuple-element.30), channel_id=1, source_target_pairs={{1,65},{3,67},{5,69},{7,71},{8,24},{10,26},{12,28},{14,30},{16,80}... | collective-permute-start | bytes 1179656 | tf_op jit(solution)/shard_map/ppermute | solution.py:193
  17.9 5.7 %collective-permute-done.2.near_raw = bf16[1024,768]{1,0:T(8,128)(2,1)S(1)} collective-permute-done((bf16[1024,768]{1,0:T(8,128)(2,1)}, bf16[1024,768]{1,0:T(8,128)(2,1)S(1)}, u32[]{:S(2)}, u32[]{:S(2)}) %collective-permute-start.2) | collective-permute-done | bytes 1572896 | tf_op jit(solution)/shard_map/ppermute | solution.py:183
  23.6 0.7 collective-permute-start.5
  24.3 20.3 %collective-permute-done.3.far_raw = bf16[1024,768]{1,0:T(8,128)(2,1)S(1)} collective-permute-done((bf16[1024,768]{1,0:T(8,128)(2,1)}, bf16[1024,768]{1,0:T(8,128)(2,1)S(1)}, u32[]{:S(2)}, u32[]{:S(2)}) %collective-permute-start.3) | collective-permute-done | bytes 1572896 | tf_op jit(solution)/shard_map/ppermute | solution.py:184
  44.6 4.2 %shard_map.18 = (f32[8,128]{1,0:T(8,128)S(1)}, f32[8,128]{1,0:T(8,128)S(1)}, f32[8,128]{1,0:T(8,128)S(1)}) custom-call(bf16[1024,768]{1,0:T(8,128)(2,1)S(1)} %get-tuple-element.22.normed, bf16[1024,768]{1,0:T(8,128)(2,1)S(1)} %collective-permute-done.2.near_raw, bf16[1024,768]{1,0:T(8,128)(2,1)S(1)} %collective-permute-done.3.far_raw, ...), custom_call_target="tpu_custom_call" | custom-call | flops 3221225472 | bytes 4734976 | tf_op jit(solution)/shard_map/pallas_call | solution.py:161
  48.8 0.0 collective-permute-done.near_raw
  48.8 0.0 collective-permute-done.1.far_raw
  48.8 0.0 collective-permute-done.4.near_raw
  48.8 0.0 collective-permute-done.5.far_raw
  48.9 0.1 collective-permute-start.6
  49.0 4.0 %collective-permute-start.7 = (f32[8,128]{1,0:T(8,128)S(1)}, f32[8,128]{1,0:T(8,128)S(1)}, u32[]{:S(2)}, u32[]{:S(2)}) collective-permute-start(f32[8,128]{1,0:T(8,128)S(1)} %get-tuple-element.36), channel_id=1, source_target_pairs={{49,1},{51,3},{53,5},{55,7},{200,8},{202,10},{204,12},{206,14},{32... | collective-permute-start | bytes 12296 | tf_op jit(solution)/shard_map/ppermute | solution.py:217
  53.0 0.0 collective-permute-done.6.from_near
  53.0 1.0 %collective-permute-done.7.from_far = f32[8,128]{1,0:T(8,128)S(1)} collective-permute-done((f32[8,128]{1,0:T(8,128)S(1)}, f32[8,128]{1,0:T(8,128)S(1)}, u32[]{:S(2)}, u32[]{:S(2)}) %collective-permute-start.7) | collective-permute-done | bytes 4128 | tf_op jit(solution)/shard_map/ppermute | solution.py:217
  54.0 0.1 shard_map.21
  54.1 32.2 %all_to_all.11 = f32[256,1,128]{2,1,0:T(1,128)S(1)} all-to-all(f32[256,1,128]{2,1,0:T(1,128)S(1)} %bitcast.6), channel_id=1, replica_groups=mesh['dev'=256] {'dev'}, dimensions={0} | all-to-all | bytes 262144 | tf_op jit(solution)/shard_map/all_to_all | solution.py:221
  86.3 0.6 shard_map.22
  (2 shorter events, 0.0 us)
Async XLA Ops:
  0.0 23.6 %collective-permute-start.2 = (bf16[1024,768]{1,0:T(8,128)(2,1)}, bf16[1024,768]{1,0:T(8,128)(2,1)S(1)}, u32[]{:S(2)}, u32[]{:S(2)}) collective-permute-start(bf16[1024,768]{1,0:T(8,128)(2,1)} %raw.1), channel_id=1, source_target_pairs={{0,16},{2,18},{4,20},{6,22},{9,73},{11,75},{13,77},{15,79},{17,1},... | collective-permute-start | bytes 4718600 | tf_op jit(solution)/shard_map/ppermute | solution.py:183
  1.3 43.3 %collective-permute-start.3 = (bf16[1024,768]{1,0:T(8,128)(2,1)}, bf16[1024,768]{1,0:T(8,128)(2,1)S(1)}, u32[]{:S(2)}, u32[]{:S(2)}) collective-permute-start(bf16[1024,768]{1,0:T(8,128)(2,1)} %raw.1), channel_id=1, source_target_pairs={{1,49},{3,51},{5,53},{7,55},{8,200},{10,202},{12,204},{14,206},{16... | collective-permute-start | bytes 4718600 | tf_op jit(solution)/shard_map/ppermute | solution.py:184
  10.1 1.4 %copy-start = (bf16[1024,768]{1,0:T(8,128)(2,1)S(1)}, bf16[1024,768]{1,0:T(8,128)(2,1)}, u32[]{:S(2)}) copy-start(bf16[1024,768]{1,0:T(8,128)(2,1)} %raw.1) | copy-start | bytes 4718596
  13.8 35.0 %collective-permute-start = (bf16[768,768]{1,0:T(8,128)(2,1)S(1)}, bf16[768,768]{1,0:T(8,128)(2,1)S(1)}, u32[]{:S(2)}, u32[]{:S(2)}) collective-permute-start(bf16[768,768]{1,0:T(8,128)(2,1)S(1)} %get-tuple-element.23), channel_id=1, source_target_pairs={{1,65},{3,67},{5,69},{7,71},{8,24},{10,26},{12,28},{14,30},{16,80}... | collective-permute-start | bytes 3538952 | tf_op jit(solution)/shard_map/ppermute | solution.py:191
  15.2 33.6 %collective-permute-start.1 = (bf16[768,768]{1,0:T(8,128)(2,1)S(1)}, bf16[768,768]{1,0:T(8,128)(2,1)S(1)}, u32[]{:S(2)}, u32[]{:S(2)}) collective-permute-start(bf16[768,768]{1,0:T(8,128)(2,1)S(1)} %get-tuple-element.23), channel_id=1, source_target_pairs={{0,192},{2,194},{4,196},{6,198},{9,57},{11,59},{13,61},{15,63},{17... | collective-permute-start | bytes 3538952 | tf_op jit(solution)/shard_map/ppermute | solution.py:192
  15.9 32.9 %collective-permute-start.4 = (bf16[256,768]{1,0:T(8,128)(2,1)S(1)}, bf16[256,768]{1,0:T(8,128)(2,1)S(1)}, u32[]{:S(2)}, u32[]{:S(2)}) collective-permute-start(bf16[256,768]{1,0:T(8,128)(2,1)S(1)} %get-tuple-element.30), channel_id=1, source_target_pairs={{1,65},{3,67},{5,69},{7,71},{8,24},{10,26},{12,28},{14,30},{16,80}... | collective-permute-start | bytes 1179656 | tf_op jit(solution)/shard_map/ppermute | solution.py:193
  23.6 25.3 %collective-permute-start.5 = (bf16[256,768]{1,0:T(8,128)(2,1)S(1)}, bf16[256,768]{1,0:T(8,128)(2,1)S(1)}, u32[]{:S(2)}, u32[]{:S(2)}) collective-permute-start(bf16[256,768]{1,0:T(8,128)(2,1)S(1)} %get-tuple-element.30), channel_id=1, source_target_pairs={{0,192},{2,194},{4,196},{6,198},{9,57},{11,59},{13,61},{15,63},{17... | collective-permute-start | bytes 1179656 | tf_op jit(solution)/shard_map/ppermute | solution.py:194
  48.9 4.1 %collective-permute-start.6 = (f32[8,128]{1,0:T(8,128)S(1)}, f32[8,128]{1,0:T(8,128)S(1)}, u32[]{:S(2)}, u32[]{:S(2)}) collective-permute-start(f32[8,128]{1,0:T(8,128)S(1)} %get-tuple-element.35), channel_id=1, source_target_pairs={{16,0},{18,2},{20,4},{22,6},{73,9},{75,11},{77,13},{79,15},{1,17},... | collective-permute-start | bytes 12296 | tf_op jit(solution)/shard_map/ppermute | solution.py:216
  49.0 5.0 %collective-permute-start.7 = (f32[8,128]{1,0:T(8,128)S(1)}, f32[8,128]{1,0:T(8,128)S(1)}, u32[]{:S(2)}, u32[]{:S(2)}) collective-permute-start(f32[8,128]{1,0:T(8,128)S(1)} %get-tuple-element.36), channel_id=1, source_target_pairs={{49,1},{51,3},{53,5},{55,7},{200,8},{202,10},{204,12},{206,14},{32... | collective-permute-start | bytes 12296 | tf_op jit(solution)/shard_map/ppermute | solution.py:217

commit v3 on v2

--- a/solution.py
+++ b/solution.py
@@ -91,10 +91,13 @@
         put(col_out, col_start, jnp.sum(total, axis=0, keepdims=True), col_add)
 
 
-def own_kernel(raw, normed, first, second, density):
-    unit_rows(raw, normed)
+def gate_kernel(raw, arrived, density, first, second):
     first[...] = raw[pl.ds(0, LATE), :]
     second[...] = raw[pl.ds(LATE, raw.shape[0] - LATE), :]
+
+
+def own_kernel(raw, normed, density):
+    unit_rows(raw, normed)
     tile_sums(normed, normed, density, 0, False, None, 0, False)
 
 
@@ -154,14 +157,15 @@
     keep[...] = weights[...] * rows / total
 
 
-def call(kernel, operands, outs, scratch=(), flops=0):
+def call(kernel, operands, outs, scratch=(), flops=0, whole=()):
     space = pl.BlockSpec(memory_space=pltpu.VMEM)
+    anywhere = pl.BlockSpec(memory_space=pl.ANY)
     shapes = [jax.ShapeDtypeStruct(*out) for out in outs]
     moved = sum(math.prod(s.shape) * s.dtype.itemsize for s in [*operands, *shapes])
     return pl.pallas_call(
         kernel,
         out_shape=shapes,
-        in_specs=[space] * len(operands),
+        in_specs=[anywhere if i in whole else space for i in range(len(operands))],
         out_specs=[space] * len(shapes),
         scratch_shapes=[pltpu.VMEM(*s) for s in scratch],
         cost_estimate=pl.CostEstimate(
@@ -182,11 +186,14 @@
 
     near_early = lax.ppermute(embeddings, "dev", near[0])
     far_early = lax.ppermute(embeddings, "dev", far[0])
-    normed, first, second, density = call(
-        own_kernel,
-        [embeddings],
-        [((rows, width), bf16), ((LATE, width), bf16), ((rest, width), bf16), sums],
-        flops=tile,
+    normed, density = call(
+        own_kernel, [embeddings], [((rows, width), bf16), sums], flops=tile
+    )
+    first, second = call(
+        gate_kernel,
+        [embeddings, near_early, density],
+        [((LATE, width), bf16), ((rest, width), bf16)],
+        whole=(1, 2),
     )
     near_first = lax.ppermute(first, "dev", near[1])
     far_first = lax.ppermute(first, "dev", far[1])

time: 87.2 us -> 84.5 us (0.969)
  starting transfers between devices: 18.9 us -> 28.8 us
  waiting for transfers between devices: 27 us -> 18.1 us
  blocking collectives: 32.2 us -> 28.2 us
    ppermute x1, waiting for transfers between devices: 20.3 us -> 0.01 us  [shards(): far_early = lax.ppermute(embeddings, 'dev', far[0])]
    ppermute x1, waiting for transfers between devices: 0.01 us -> 4.21 us  [shards(): near_second = lax.ppermute(second, 'dev', near[1])]
    ppermute x1, starting transfers between devices: 0.08 us -> 4.25 us  [shards(): from_near = lax.ppermute(to_near, 'dev', inverse(near[0] + near[1]))]
    all_to_all x1, blocking collectives: 32.2 us -> 28.2 us  [shards(): totals = lax.all_to_all(total, 'dev', 0, 0, tiled=True)]
    ppermute x1, waiting for transfers between devices: 5.67 us -> 9.31 us  [shards(): near_early = lax.ppermute(embeddings, 'dev', near[0])]
    ppermute x1, waiting for transfers between devices: 0.01 us -> 3.61 us  [shards(): near_first = lax.ppermute(first, 'dev', near[1])]
    ppermute x1, starting transfers between devices: 1.36 us -> 3.47 us  [shards(): near_first = lax.ppermute(first, 'dev', near[1])]
    ppermute x1, starting transfers between devices: 4 us -> 6.01 us  [shards(): from_far = lax.ppermute(to_far, 'dev', inverse(far[0] + far[1]))]
  transfers between devices with their start and end apart: 8 -> 8, of which waited for: 3 -> 4; matrix products, arithmetic and copies ran while one was open for 0% -> 0% of each run, Pallas kernels for 8% -> 8%
where the time goes in v3:
time: 84.5 us; the launch traced here: 84.2 us
  starting transfers between devices  28.8 us (34%)
  blocking collectives  28.2 us (33%)
  waiting for transfers between devices  18.1 us (21%)
  Pallas kernels  7.56 us (9%)
  local copies, waits for them, and re-layouts  1.41 us (2%)
    all_to_all x1, blocking collectives, shards(): totals = lax.all_to_all(total, 'dev', 0, 0, tiled=True)  28.2 us
    ppermute x1, waiting for transfers between devices, shards(): near_early = lax.ppermute(embeddings, 'dev', near[0])  9.31 us
    ppermute x1, starting transfers between devices, shards(): far_early = lax.ppermute(embeddings, 'dev', far[0])  8.76 us
    pallas_call x7, Pallas kernels, call(): pl.pallas_call(kernel, out_shape=shapes, in_specs=[anywhere if i in whole...  7.56 us
    ppermute x1, starting transfers between devices, shards(): from_far = lax.ppermute(to_far, 'dev', inverse(far[0] + far[1]))  6.01 us
    ppermute x1, starting transfers between devices, shards(): from_near = lax.ppermute(to_near, 'dev', inverse(near[0] + near[1]))  4.25 us
    ppermute x1, waiting for transfers between devices, shards(): near_second = lax.ppermute(second, 'dev', near[1])  4.21 us
    ppermute x1, starting transfers between devices, shards(): near_second = lax.ppermute(second, 'dev', near[1])  3.62 us
  transfers between devices with their start and end apart: 8, of which 4 were waited for; matrix products, arithmetic and copies ran while one was open for 0% of the time, Pallas kernels for 8%

profile of v3, /device:TPU:1, one launch (start us, length us, event | category | flops | bytes accessed | tf_op | source)
XLA Modules:
  0.0 84.2 jit_solution(17644346403375428677)
XLA Ops:
  0.0 1.3 %collective-permute-start = (bf16[1024,768]{1,0:T(8,128)(2,1)}, bf16[1024,768]{1,0:T(8,128)(2,1)S(1)}, u32[]{:S(2)}, u32[]{:S(2)}) collective-permute-start(bf16[1024,768]{1,0:T(8,128)(2,1)} %raw.3), channel_id=1, source_target_pairs={{0,16},{2,18},{4,20},{6,22},{9,73},{11,75},{13,77},{15,79},{17,1},... | collective-permute-start | bytes 4718600 | tf_op jit(solution)/shard_map/ppermute | solution.py:187
  1.3 8.8 %collective-permute-start.3 = (bf16[1024,768]{1,0:T(8,128)(2,1)}, bf16[1024,768]{1,0:T(8,128)(2,1)S(1)}, u32[]{:S(2)}, u32[]{:S(2)}) collective-permute-start(bf16[1024,768]{1,0:T(8,128)(2,1)} %raw.3), channel_id=1, source_target_pairs={{1,49},{3,51},{5,53},{7,55},{8,200},{10,202},{12,204},{14,206},{16... | collective-permute-start | bytes 4718600 | tf_op jit(solution)/shard_map/ppermute | solution.py:188
  10.1 0.0 copy-start
  10.1 1.4 %copy-done = bf16[1024,768]{1,0:T(8,128)(2,1)S(1)} copy-done((bf16[1024,768]{1,0:T(8,128)(2,1)S(1)}, bf16[1024,768]{1,0:T(8,128)(2,1)}, u32[]{:S(2)}) %copy-start) | copy-done | bytes 1572888
  11.5 2.3 %shard_map.17 = (bf16[1024,768]{1,0:T(8,128)(2,1)S(1)}, f32[8,128]{1,0:T(8,128)S(1)}) custom-call(bf16[1024,768]{1,0:T(8,128)(2,1)S(1)} %copy-done), custom_call_target="tpu_custom_call" | custom-call | flops 1610612736 | bytes 3149824 | tf_op jit(solution)/shard_map/pallas_call | solution.py:165
  13.8 9.3 %collective-permute-done.arrived.near_raw = bf16[1024,768]{1,0:T(8,128)(2,1)S(1)} collective-permute-done((bf16[1024,768]{1,0:T(8,128)(2,1)}, bf16[1024,768]{1,0:T(8,128)(2,1)S(1)}, u32[]{:S(2)}, u32[]{:S(2)}) %collective-permute-start) | collective-permute-done | bytes 1572896 | tf_op jit(solution)/shard_map/ppermute | solution.py:187
  23.1 0.1 shard_map.18
  23.2 3.5 %collective-permute-start.1 = (bf16[768,768]{1,0:T(8,128)(2,1)S(1)}, bf16[768,768]{1,0:T(8,128)(2,1)S(1)}, u32[]{:S(2)}, u32[]{:S(2)}) collective-permute-start(bf16[768,768]{1,0:T(8,128)(2,1)S(1)} %get-tuple-element.24), channel_id=1, source_target_pairs={{1,65},{3,67},{5,69},{7,71},{8,24},{10,26},{12,28},{14,30},{16,80}... | collective-permute-start | bytes 3538952 | tf_op jit(solution)/shard_map/ppermute | solution.py:198
  26.7 0.7 collective-permute-start.2
  27.4 3.6 %collective-permute-start.4 = (bf16[256,768]{1,0:T(8,128)(2,1)S(1)}, bf16[256,768]{1,0:T(8,128)(2,1)S(1)}, u32[]{:S(2)}, u32[]{:S(2)}) collective-permute-start(bf16[256,768]{1,0:T(8,128)(2,1)S(1)} %get-tuple-element.30), channel_id=1, source_target_pairs={{1,65},{3,67},{5,69},{7,71},{8,24},{10,26},{12,28},{14,30},{16,80}... | collective-permute-start | bytes 1179656 | tf_op jit(solution)/shard_map/ppermute | solution.py:200
  31.1 0.7 collective-permute-start.5
  31.8 0.0 collective-permute-done.3.far_raw
  31.8 4.4 %shard_map.19 = (f32[8,128]{1,0:T(8,128)S(1)}, f32[8,128]{1,0:T(8,128)S(1)}, f32[8,128]{1,0:T(8,128)S(1)}) custom-call(bf16[1024,768]{1,0:T(8,128)(2,1)S(1)} %get-tuple-element.22.normed, bf16[1024,768]{1,0:T(8,128)(2,1)S(1)} %collective-permute-done.arrived.near_raw, bf16[1024,768]{1,0:T(8,128)(2,1)S(1)} %collective-permute-done.3.far_raw, ...), custom_call_target="tpu_custom_call" | custom-call | flops 3221225472 | bytes 4734976 | tf_op jit(solution)/shard_map/pallas_call | solution.py:165
  36.1 3.6 %collective-permute-done.1.near_raw = bf16[768,768]{1,0:T(8,128)(2,1)S(1)} collective-permute-done((bf16[768,768]{1,0:T(8,128)(2,1)S(1)}, bf16[768,768]{1,0:T(8,128)(2,1)S(1)}, u32[]{:S(2)}, u32[]{:S(2)}) %collective-permute-start.1) | collective-permute-done | bytes 1179680 | tf_op jit(solution)/shard_map/ppermute | solution.py:198
  39.7 0.0 collective-permute-done.2.far_raw
  39.7 4.2 %collective-permute-done.4.near_raw = bf16[256,768]{1,0:T(8,128)(2,1)S(1)} collective-permute-done((bf16[256,768]{1,0:T(8,128)(2,1)S(1)}, bf16[256,768]{1,0:T(8,128)(2,1)S(1)}, u32[]{:S(2)}, u32[]{:S(2)}) %collective-permute-start.4) | collective-permute-done | bytes 393248 | tf_op jit(solution)/shard_map/ppermute | solution.py:200
  44.0 0.0 collective-permute-done.5.far_raw
  44.0 4.2 %collective-permute-start.6 = (f32[8,128]{1,0:T(8,128)S(1)}, f32[8,128]{1,0:T(8,128)S(1)}, u32[]{:S(2)}, u32[]{:S(2)}) collective-permute-start(f32[8,128]{1,0:T(8,128)S(1)} %get-tuple-element.35), channel_id=1, source_target_pairs={{16,0},{18,2},{20,4},{22,6},{73,9},{75,11},{77,13},{79,15},{1,17},... | collective-permute-start | bytes 12296 | tf_op jit(solution)/shard_map/ppermute | solution.py:223
  48.2 6.0 %collective-permute-start.7 = (f32[8,128]{1,0:T(8,128)S(1)}, f32[8,128]{1,0:T(8,128)S(1)}, u32[]{:S(2)}, u32[]{:S(2)}) collective-permute-start(f32[8,128]{1,0:T(8,128)S(1)} %get-tuple-element.36), channel_id=1, source_target_pairs={{49,1},{51,3},{53,5},{55,7},{200,8},{202,10},{204,12},{206,14},{32... | collective-permute-start | bytes 12296 | tf_op jit(solution)/shard_map/ppermute | solution.py:224
  54.2 0.0 collective-permute-done.6.from_near
  54.2 1.0 %collective-permute-done.7.from_far = f32[8,128]{1,0:T(8,128)S(1)} collective-permute-done((f32[8,128]{1,0:T(8,128)S(1)}, f32[8,128]{1,0:T(8,128)S(1)}, u32[]{:S(2)}, u32[]{:S(2)}) %collective-permute-start.7) | collective-permute-done | bytes 4128 | tf_op jit(solution)/shard_map/ppermute | solution.py:224
  55.2 0.1 shard_map.22
  55.3 28.2 %all_to_all.11 = f32[256,1,128]{2,1,0:T(1,128)S(1)} all-to-all(f32[256,1,128]{2,1,0:T(1,128)S(1)} %bitcast.6), channel_id=1, replica_groups=mesh['dev'=256] {'dev'}, dimensions={0} | all-to-all | bytes 262144 | tf_op jit(solution)/shard_map/all_to_all | solution.py:228
  83.6 0.6 shard_map.23
  (2 shorter events, 0.0 us)
Async XLA Ops:
  0.0 23.1 %collective-permute-start = (bf16[1024,768]{1,0:T(8,128)(2,1)}, bf16[1024,768]{1,0:T(8,128)(2,1)S(1)}, u32[]{:S(2)}, u32[]{:S(2)}) collective-permute-start(bf16[1024,768]{1,0:T(8,128)(2,1)} %raw.3), channel_id=1, source_target_pairs={{0,16},{2,18},{4,20},{6,22},{9,73},{11,75},{13,77},{15,79},{17,1},... | collective-permute-start | bytes 4718600 | tf_op jit(solution)/shard_map/ppermute | solution.py:187
  1.3 30.5 %collective-permute-start.3 = (bf16[1024,768]{1,0:T(8,128)(2,1)}, bf16[1024,768]{1,0:T(8,128)(2,1)S(1)}, u32[]{:S(2)}, u32[]{:S(2)}) collective-permute-start(bf16[1024,768]{1,0:T(8,128)(2,1)} %raw.3), channel_id=1, source_target_pairs={{1,49},{3,51},{5,53},{7,55},{8,200},{10,202},{12,204},{14,206},{16... | collective-permute-start | bytes 4718600 | tf_op jit(solution)/shard_map/ppermute | solution.py:188
  10.1 1.4 %copy-start = (bf16[1024,768]{1,0:T(8,128)(2,1)S(1)}, bf16[1024,768]{1,0:T(8,128)(2,1)}, u32[]{:S(2)}) copy-start(bf16[1024,768]{1,0:T(8,128)(2,1)} %raw.3) | copy-start | bytes 4718596
  23.2 16.5 %collective-permute-start.1 = (bf16[768,768]{1,0:T(8,128)(2,1)S(1)}, bf16[768,768]{1,0:T(8,128)(2,1)S(1)}, u32[]{:S(2)}, u32[]{:S(2)}) collective-permute-start(bf16[768,768]{1,0:T(8,128)(2,1)S(1)} %get-tuple-element.24), channel_id=1, source_target_pairs={{1,65},{3,67},{5,69},{7,71},{8,24},{10,26},{12,28},{14,30},{16,80}... | collective-permute-start | bytes 3538952 | tf_op jit(solution)/shard_map/ppermute | solution.py:198
  26.7 13.1 %collective-permute-start.2 = (bf16[768,768]{1,0:T(8,128)(2,1)S(1)}, bf16[768,768]{1,0:T(8,128)(2,1)S(1)}, u32[]{:S(2)}, u32[]{:S(2)}) collective-permute-start(bf16[768,768]{1,0:T(8,128)(2,1)S(1)} %get-tuple-element.24), channel_id=1, source_target_pairs={{0,192},{2,194},{4,196},{6,198},{9,57},{11,59},{13,61},{15,63},{17... | collective-permute-start | bytes 3538952 | tf_op jit(solution)/shard_map/ppermute | solution.py:199
  27.4 16.5 %collective-permute-start.4 = (bf16[256,768]{1,0:T(8,128)(2,1)S(1)}, bf16[256,768]{1,0:T(8,128)(2,1)S(1)}, u32[]{:S(2)}, u32[]{:S(2)}) collective-permute-start(bf16[256,768]{1,0:T(8,128)(2,1)S(1)} %get-tuple-element.30), channel_id=1, source_target_pairs={{1,65},{3,67},{5,69},{7,71},{8,24},{10,26},{12,28},{14,30},{16,80}... | collective-permute-start | bytes 1179656 | tf_op jit(solution)/shard_map/ppermute | solution.py:200
  31.1 12.9 %collective-permute-start.5 = (bf16[256,768]{1,0:T(8,128)(2,1)S(1)}, bf16[256,768]{1,0:T(8,128)(2,1)S(1)}, u32[]{:S(2)}, u32[]{:S(2)}) collective-permute-start(bf16[256,768]{1,0:T(8,128)(2,1)S(1)} %get-tuple-element.30), channel_id=1, source_target_pairs={{0,192},{2,194},{4,196},{6,198},{9,57},{11,59},{13,61},{15,63},{17... | collective-permute-start | bytes 1179656 | tf_op jit(solution)/shard_map/ppermute | solution.py:201
  44.0 10.3 %collective-permute-start.6 = (f32[8,128]{1,0:T(8,128)S(1)}, f32[8,128]{1,0:T(8,128)S(1)}, u32[]{:S(2)}, u32[]{:S(2)}) collective-permute-start(f32[8,128]{1,0:T(8,128)S(1)} %get-tuple-element.35), channel_id=1, source_target_pairs={{16,0},{18,2},{20,4},{22,6},{73,9},{75,11},{77,13},{79,15},{1,17},... | collective-permute-start | bytes 12296 | tf_op jit(solution)/shard_map/ppermute | solution.py:223
  48.2 7.0 %collective-permute-start.7 = (f32[8,128]{1,0:T(8,128)S(1)}, f32[8,128]{1,0:T(8,128)S(1)}, u32[]{:S(2)}, u32[]{:S(2)}) collective-permute-start(f32[8,128]{1,0:T(8,128)S(1)} %get-tuple-element.36), channel_id=1, source_target_pairs={{49,1},{51,3},{53,5},{55,7},{200,8},{202,10},{204,12},{206,14},{32... | collective-permute-start | bytes 12296 | tf_op jit(solution)/shard_map/ppermute | solution.py:224

commit v4 on v2

v4 whole, which is shorter than its diff:
```python
import functools
import math

import jax
import jax.numpy as jnp
from jax import lax
from jax.experimental import pallas as pl
from jax.experimental.pallas import tpu as pltpu
from jax.sharding import PartitionSpec as P

ROUNDS = 4
LANES = 128
STEP = 256

sharpness = 10.0
RATE = sharpness * math.log2(math.e)


def parity(value):
    return bin(value).count("1") & 1


def plan(players):
    low = players.bit_length() - 1 - ROUNDS
    z_near, z_swap = 1 << low, 3 << low
    x_near, x_swap = 4 << low, 12 << low
    near, far = [], []
    for player in range(players):
        if parity(player >> low) ^ (player & 1):
            near.append((player, player ^ x_near))
            far.append((player, player ^ z_swap))
        else:
            near.append((player, player ^ z_near))
            far.append((player, player ^ x_swap))
    return near, far


def inverse(pairs):
    return [(target, source) for source, target in pairs]


def unit(values):
    widened = values.astype(jnp.float32)
    mean = jnp.mean(widened * widened, axis=1, keepdims=True)
    scale = lax.rsqrt(mean + 1e-06) * (1.0 / math.sqrt(values.shape[1]))
    return (widened * scale).astype(jnp.bfloat16)


def unit_rows(source, target):
    rows = source.shape[0]
    for start in range(0, rows, STEP):
        part = pl.ds(start, min(STEP, rows - start))
        target[part, :] = unit(source[part, :])


def put(target, start, vector, add):
    for k in range(vector.shape[1] // LANES):
        at = pl.ds(start // LANES + k, 1)
        part = vector[:, k * LANES : (k + 1) * LANES]
        target[at, :] = target[at, :] + part if add else part


def tile_sums(left, right, row_out, row_start, row_add, col_out, col_start, col_add):
    rows, cols = left.shape[0], right.shape[0]
    total = None
    for start in range(0, rows, STEP):
        similarity = lax.dot_general(
            left[pl.ds(start, STEP), :],
            right[...],
            (((1,), (1,)), ((), ())),
            preferred_element_type=jnp.float32,
        )
        value = jnp.exp2(similarity * RATE - RATE)
        folded = value[:, :LANES]
        for k in range(1, cols // LANES):
            folded = folded + value[:, k * LANES : (k + 1) * LANES]
        sums = jnp.sum(folded.T, axis=0, keepdims=True)
        put(row_out, row_start + start, sums, row_add)
        if col_out is not None:
            part = jnp.sum(value.reshape(STEP // 8, 8, cols), axis=0)
            total = part if total is None else total + part
    if col_out is not None:
        put(col_out, col_start, jnp.sum(total, axis=0, keepdims=True), col_add)


def own_kernel(raw, normed, density):
    unit_rows(raw, normed)
    tile_sums(normed, normed, density, 0, False, None, 0, False)


def near_kernel(normed, raw, density, density_out, to_near, near):
    unit_rows(raw, near)
    density_out[...] = density[...]
    tile_sums(normed, near, density_out, 0, True, to_near, 0, False)


def far_kernel(near, raw, to_near, near_out, to_far, far):
    unit_rows(raw, far)
    near_out[...] = to_near[...]
    tile_sums(near, far, near_out, 0, True, to_far, 0, False)


def weight_kernel(density, from_near, from_far, weights, total):
    value = 1.0 / (density[...] + from_near[...] + from_far[...])
    weights[...] = value
    total[...] = jnp.full(total.shape, jnp.sum(value))


def scale_kernel(weights, totals, keep, *, rows):
    total = jnp.sum(totals[...], axis=0, keepdims=True)
    keep[...] = weights[...] * rows / total


def call(kernel, operands, outs, scratch=(), flops=0):
    space = pl.BlockSpec(memory_space=pltpu.VMEM)
    shapes = [jax.ShapeDtypeStruct(*out) for out in outs]
    moved = sum(math.prod(s.shape) * s.dtype.itemsize for s in [*operands, *shapes])
    return pl.pallas_call(
        kernel,
        out_shape=shapes,
        in_specs=[space] * len(operands),
        out_specs=[space] * len(shapes),
        scratch_shapes=[pltpu.VMEM(*s) for s in scratch],
        cost_estimate=pl.CostEstimate(
            flops=flops, bytes_accessed=moved, transcendentals=0
        ),
        compiler_params=pltpu.CompilerParams(vmem_limit_bytes=32 * 2**20),
    )(*operands)


def shards(embeddings):
    players = lax.axis_size("dev")
    rows, width = embeddings.shape
    bf16, f32 = jnp.bfloat16, jnp.float32
    block, sums = ((rows, width), bf16), ((rows // LANES, LANES), f32)
    tile = 2 * rows * rows * width
    near_pairs, far_pairs = plan(players)

    near = lax.ppermute(embeddings, "dev", near_pairs)
    far = lax.ppermute(embeddings, "dev", far_pairs)
    normed, density = call(own_kernel, [embeddings], [block, sums], flops=tile)
    density, to_near, near = call(
        near_kernel, [normed, near, density], [sums, sums, block], flops=tile
    )
    to_near, to_far = call(
        far_kernel, [near, far, to_near], [sums, sums], [block], flops=tile
    )
    from_near = lax.ppermute(to_near, "dev", inverse(near_pairs))
    from_far = lax.ppermute(to_far, "dev", inverse(far_pairs))
    weights, total = call(
        weight_kernel, [density, from_near, from_far], [sums, ((players, LANES), f32)]
    )
    totals = lax.all_to_all(total, "dev", 0, 0, tiled=True)
    (keep,) = call(
        functools.partial(scale_kernel, rows=float(players * rows)), [weights, totals], [sums]
    )
    return keep.reshape(rows)


def solution(mesh):
    return jax.shard_map(
        shards,
        mesh=mesh,
        in_specs=(P("dev", None),),
        out_specs=P("dev"),
        check_vma=False,
    )
```

time: 87.2 us -> 78 us (0.89)
  starting transfers between devices: 18.9 us -> 12.1 us
  blocking collectives: 32.2 us -> 27.1 us
  waiting for transfers between devices: 27 us -> 29.4 us
    ppermute x8 -> x4, starting transfers between devices: 18.9 us -> 12.1 us  [the longest x1 6.02 us: shards(): far = lax.ppermute(embeddings, 'dev', far_pairs)]
    all_to_all x1, blocking collectives: 32.2 us -> 27.1 us  [shards(): totals = lax.all_to_all(total, 'dev', 0, 0, tiled=True)]
    ppermute x8 -> x4, waiting for transfers between devices: 27 us -> 29.4 us  [the longest x1 27.1 us: shards(): near = lax.ppermute(embeddings, 'dev', near_pairs)]
    pallas_call x6 -> x5, Pallas kernels: 7.37 us -> 7.79 us  [call(): pl.pallas_call(kernel, out_shape=shapes, in_specs=[space] * len(operands)...]
  transfers between devices with their start and end apart: 8 -> 4, of which waited for: 3 -> 3; matrix products, arithmetic and copies ran while one was open for 0% -> 0% of each run, Pallas kernels for 8% -> 6%
where the time goes in v4:
time: 78 us; the launch traced here: 77.8 us
  waiting for transfers between devices  29.4 us (38%)
  blocking collectives  27.1 us (35%)
  starting transfers between devices  12.1 us (16%)
  Pallas kernels  7.79 us (10%)
  local copies, waits for them, and re-layouts  1.44 us (2%)
    ppermute x1, waiting for transfers between devices, shards(): near = lax.ppermute(embeddings, 'dev', near_pairs)  27.1 us
    all_to_all x1, blocking collectives, shards(): totals = lax.all_to_all(total, 'dev', 0, 0, tiled=True)  27.1 us
    pallas_call x5, Pallas kernels, call(): pl.pallas_call(kernel, out_shape=shapes, in_specs=[space] * len(operands)...  7.79 us
    ppermute x1, starting transfers between devices, shards(): far = lax.ppermute(embeddings, 'dev', far_pairs)  6.02 us
    ppermute x1, starting transfers between devices, shards(): from_far = lax.ppermute(to_far, 'dev', inverse(far_pairs))  3.96 us
    ppermute x1, starting transfers between devices, shards(): near = lax.ppermute(embeddings, 'dev', near_pairs)  2.04 us
  transfers between devices with their start and end apart: 4, of which 3 were waited for; matrix products, arithmetic and copies ran while one was open for 0% of the time, Pallas kernels for 6%

profile of v4, /device:TPU:1, one launch (start us, length us, event | category | flops | bytes accessed | tf_op | source)
XLA Modules:
  0.0 77.8 jit_solution(14622876935982175332)
XLA Ops:
  0.0 2.0 %collective-permute-start = (bf16[1024,768]{1,0:T(8,128)(2,1)}, bf16[1024,768]{1,0:T(8,128)(2,1)S(1)}, u32[]{:S(2)}, u32[]{:S(2)}) collective-permute-start(bf16[1024,768]{1,0:T(8,128)(2,1)} %raw.1), channel_id=1, source_target_pairs={{0,16},{1,65},{2,18},{3,67},{4,20},{5,69},{6,22},{7,71},{8,24},{9,... | collective-permute-start | bytes 4718600 | tf_op jit(solution)/shard_map/ppermute | solution.py:139
  2.0 6.0 %collective-permute-start.1 = (bf16[1024,768]{1,0:T(8,128)(2,1)}, bf16[1024,768]{1,0:T(8,128)(2,1)S(1)}, u32[]{:S(2)}, u32[]{:S(2)}) collective-permute-start(bf16[1024,768]{1,0:T(8,128)(2,1)} %raw.1), channel_id=1, source_target_pairs={{0,192},{1,49},{2,194},{3,51},{4,196},{5,53},{6,198},{7,55},{8,200... | collective-permute-start | bytes 4718600 | tf_op jit(solution)/shard_map/ppermute | solution.py:140
  8.1 0.0 copy-start
  8.1 1.4 %copy-done = bf16[1024,768]{1,0:T(8,128)(2,1)S(1)} copy-done((bf16[1024,768]{1,0:T(8,128)(2,1)S(1)}, bf16[1024,768]{1,0:T(8,128)(2,1)}, u32[]{:S(2)}) %copy-start) | copy-done | bytes 1572888
  9.5 2.3 %shard_map.17 = (bf16[1024,768]{1,0:T(8,128)(2,1)S(1)}, f32[8,128]{1,0:T(8,128)S(1)}) custom-call(bf16[1024,768]{1,0:T(8,128)(2,1)S(1)} %copy-done), custom_call_target="tpu_custom_call" | custom-call | flops 1610612736 | bytes 3149824 | tf_op jit(solution)/shard_map/pallas_call | solution.py:118
  11.8 27.1 %collective-permute-done.raw = bf16[1024,768]{1,0:T(8,128)(2,1)S(1)} collective-permute-done((bf16[1024,768]{1,0:T(8,128)(2,1)}, bf16[1024,768]{1,0:T(8,128)(2,1)S(1)}, u32[]{:S(2)}, u32[]{:S(2)}) %collective-permute-start) | collective-permute-done | bytes 1572896 | tf_op jit(solution)/shard_map/ppermute | solution.py:139
  38.9 2.4 %shard_map.18 = (f32[8,128]{1,0:T(8,128)S(1)}, f32[8,128]{1,0:T(8,128)S(1)}, bf16[1024,768]{1,0:T(8,128)(2,1)S(1)}) custom-call(bf16[1024,768]{1,0:T(8,128)(2,1)S(1)} %get-tuple-element.14.normed, bf16[1024,768]{1,0:T(8,128)(2,1)S(1)} %collective-permute-done.raw, f32[8,128]{1,0:T(8,128)S(1)} %get-tuple-element.15.density), custom_call_target="tpu_custom_call" | custom-call | flops 1610612736 | bytes 4730880 | tf_op jit(solution)/shard_map/pallas_call | solution.py:118
  41.3 1.3 %collective-permute-done.1.raw = bf16[1024,768]{1,0:T(8,128)(2,1)S(1)} collective-permute-done((bf16[1024,768]{1,0:T(8,128)(2,1)}, bf16[1024,768]{1,0:T(8,128)(2,1)S(1)}, u32[]{:S(2)}, u32[]{:S(2)}) %collective-permute-start.1) | collective-permute-done | bytes 1572896 | tf_op jit(solution)/shard_map/ppermute | solution.py:140
  42.6 2.3 %shard_map.19 = (f32[8,128]{1,0:T(8,128)S(1)}, f32[8,128]{1,0:T(8,128)S(1)}) custom-call(bf16[1024,768]{1,0:T(8,128)(2,1)S(1)} %get-tuple-element.17.near, bf16[1024,768]{1,0:T(8,128)(2,1)S(1)} %collective-permute-done.1.raw, f32[8,128]{1,0:T(8,128)S(1)} %get-tuple-element.18.to_near), custom_call_target="tpu_custom_call" | custom-call | flops 1610612736 | bytes 3158016 | tf_op jit(solution)/shard_map/pallas_call | solution.py:118
  44.9 0.1 collective-permute-start.2
  45.0 4.0 %collective-permute-start.3 = (f32[8,128]{1,0:T(8,128)S(1)}, f32[8,128]{1,0:T(8,128)S(1)}, u32[]{:S(2)}, u32[]{:S(2)}) collective-permute-start(f32[8,128]{1,0:T(8,128)S(1)} %get-tuple-element.20), channel_id=1, source_target_pairs={{192,0},{49,1},{194,2},{51,3},{196,4},{53,5},{198,6},{55,7},{200,8... | collective-permute-start | bytes 12296 | tf_op jit(solution)/shard_map/ppermute | solution.py:149
  49.0 0.0 collective-permute-done.2.from_near
  49.0 1.0 %collective-permute-done.3.from_far = f32[8,128]{1,0:T(8,128)S(1)} collective-permute-done((f32[8,128]{1,0:T(8,128)S(1)}, f32[8,128]{1,0:T(8,128)S(1)}, u32[]{:S(2)}, u32[]{:S(2)}) %collective-permute-start.3) | collective-permute-done | bytes 4128 | tf_op jit(solution)/shard_map/ppermute | solution.py:149
  50.0 0.1 shard_map.20
  50.1 27.1 %all_to_all.11 = f32[256,1,128]{2,1,0:T(1,128)S(1)} all-to-all(f32[256,1,128]{2,1,0:T(1,128)S(1)} %bitcast.6), channel_id=1, replica_groups=mesh['dev'=256] {'dev'}, dimensions={0} | all-to-all | bytes 262144 | tf_op jit(solution)/shard_map/all_to_all | solution.py:153
  77.2 0.6 shard_map.21
Async XLA Ops:
  0.0 38.9 %collective-permute-start = (bf16[1024,768]{1,0:T(8,128)(2,1)}, bf16[1024,768]{1,0:T(8,128)(2,1)S(1)}, u32[]{:S(2)}, u32[]{:S(2)}) collective-permute-start(bf16[1024,768]{1,0:T(8,128)(2,1)} %raw.1), channel_id=1, source_target_pairs={{0,16},{1,65},{2,18},{3,67},{4,20},{5,69},{6,22},{7,71},{8,24},{9,... | collective-permute-start | bytes 4718600 | tf_op jit(solution)/shard_map/ppermute | solution.py:139
  2.0 40.6 %collective-permute-start.1 = (bf16[1024,768]{1,0:T(8,128)(2,1)}, bf16[1024,768]{1,0:T(8,128)(2,1)S(1)}, u32[]{:S(2)}, u32[]{:S(2)}) collective-permute-start(bf16[1024,768]{1,0:T(8,128)(2,1)} %raw.1), channel_id=1, source_target_pairs={{0,192},{1,49},{2,194},{3,51},{4,196},{5,53},{6,198},{7,55},{8,200... | collective-permute-start | bytes 4718600 | tf_op jit(solution)/shard_map/ppermute | solution.py:140
  8.1 1.4 %copy-start = (bf16[1024,768]{1,0:T(8,128)(2,1)S(1)}, bf16[1024,768]{1,0:T(8,128)(2,1)}, u32[]{:S(2)}) copy-start(bf16[1024,768]{1,0:T(8,128)(2,1)} %raw.1) | copy-start | bytes 4718596
  44.9 4.1 %collective-permute-start.2 = (f32[8,128]{1,0:T(8,128)S(1)}, f32[8,128]{1,0:T(8,128)S(1)}, u32[]{:S(2)}, u32[]{:S(2)}) collective-permute-start(f32[8,128]{1,0:T(8,128)S(1)} %get-tuple-element.19), channel_id=1, source_target_pairs={{16,0},{65,1},{18,2},{67,3},{20,4},{69,5},{22,6},{71,7},{24,8},{73... | collective-permute-start | bytes 12296 | tf_op jit(solution)/shard_map/ppermute | solution.py:148
  45.0 5.0 %collective-permute-start.3 = (f32[8,128]{1,0:T(8,128)S(1)}, f32[8,128]{1,0:T(8,128)S(1)}, u32[]{:S(2)}, u32[]{:S(2)}) collective-permute-start(f32[8,128]{1,0:T(8,128)S(1)} %get-tuple-element.20), channel_id=1, source_target_pairs={{192,0},{49,1},{194,2},{51,3},{196,4},{53,5},{198,6},{55,7},{200,8... | collective-permute-start | bytes 12296 | tf_op jit(solution)/shard_map/ppermute | solution.py:149

commit v5 on v4

--- a/solution.py
+++ b/solution.py
@@ -24,19 +24,22 @@
     low = players.bit_length() - 1 - ROUNDS
     z_near, z_swap = 1 << low, 3 << low
     x_near, x_swap = 4 << low, 12 << low
-    near, far = [], []
+    pairs = [], [], [], []
     for player in range(players):
-        if parity(player >> low) ^ (player & 1):
-            near.append((player, player ^ x_near))
-            far.append((player, player ^ z_swap))
-        else:
-            near.append((player, player ^ z_near))
-            far.append((player, player ^ x_swap))
-    return near, far
+        z_holder = parity(player >> low) ^ (player & 1)
+        pairs[0 if not z_holder else 2].append((player, player ^ (x_near if z_holder else z_near)))
+        pairs[1 if z_holder else 3].append((player, player ^ (z_swap if z_holder else x_swap)))
+    return pairs
 
 
 def inverse(pairs):
     return [(target, source) for source, target in pairs]
+
+
+def holds_z():
+    me = lax.axis_index("dev")
+    bits = me ^ (me >> 4) ^ (me >> 5) ^ (me >> 6) ^ (me >> 7)
+    return lax.rem(bits, 2) == 1
 
 
 def unit(values):
@@ -88,27 +91,70 @@
     tile_sums(normed, normed, density, 0, False, None, 0, False)
 
 
-def near_kernel(normed, raw, density, density_out, to_near, near):
-    unit_rows(raw, near)
+def x_kernel(normed, near_raw, far_raw, density, density_out, to_near, to_far, near, far):
     density_out[...] = density[...]
-    tile_sums(normed, near, density_out, 0, True, to_near, 0, False)
-
-
-def far_kernel(near, raw, to_near, near_out, to_far, far):
-    unit_rows(raw, far)
-    near_out[...] = to_near[...]
-    tile_sums(near, far, near_out, 0, True, to_far, 0, False)
-
-
-def weight_kernel(density, from_near, from_far, weights, total):
-    value = 1.0 / (density[...] + from_near[...] + from_far[...])
-    weights[...] = value
-    total[...] = jnp.full(total.shape, jnp.sum(value))
-
-
-def scale_kernel(weights, totals, keep, *, rows):
+
+    @pl.when(jnp.logical_not(holds_z()))
+    def _():
+        unit_rows(near_raw, near)
+        unit_rows(far_raw, far)
+        tile_sums(normed, near, density_out, 0, True, to_near, 0, False)
+        tile_sums(near, far, to_near, 0, True, to_far, 0, False)
+
+    @pl.when(holds_z())
+    def _():
+        to_near[...] = jnp.zeros_like(to_near)
+        to_far[...] = jnp.zeros_like(to_far)
+
+
+def add_kernel(first, second, third, out):
+    out[...] = first[...] + second[...] + third[...]
+
+
+def near_kernel(raw, part, near):
+    @pl.when(holds_z())
+    def _():
+        unit_rows(raw, near)
+
+
+def far_kernel(near, raw, part, part_out, to_far, far):
+    part_out[...] = part[...]
+
+    @pl.when(holds_z())
+    def _():
+        unit_rows(raw, far)
+        tile_sums(near, far, part_out, 0, True, to_far, 0, False)
+
+
+def own_near_kernel(normed, near, density, part, density_out, part_out):
+    density_out[...] = density[...]
+    part_out[...] = part[...]
+
+    @pl.when(holds_z())
+    def _():
+        tile_sums(normed, near, density_out, 0, True, part_out, 0, True)
+
+
+def weight_kernel(density, part, from_far, weights, near_weights, total):
+    own = 1.0 / (density[...] + from_far[...])
+    weights[...] = own
+
+    @pl.when(holds_z())
+    def _():
+        near = 1.0 / part[...]
+        near_weights[...] = near
+        total[...] = jnp.full(total.shape, jnp.sum(own + near))
+
+    @pl.when(jnp.logical_not(holds_z()))
+    def _():
+        near_weights[...] = jnp.zeros_like(near_weights)
+        total[...] = jnp.zeros_like(total)
+
+
+def scale_kernel(weights, sent_weights, totals, keep, *, rows):
     total = jnp.sum(totals[...], axis=0, keepdims=True)
-    keep[...] = weights[...] * rows / total
+    value = jnp.where(holds_z(), weights[...], sent_weights[...])
+    keep[...] = value * rows / total
 
 
 def call(kernel, operands, outs, scratch=(), flops=0):
@@ -134,25 +180,43 @@
     bf16, f32 = jnp.bfloat16, jnp.float32
     block, sums = ((rows, width), bf16), ((rows // LANES, LANES), f32)
     tile = 2 * rows * rows * width
-    near_pairs, far_pairs = plan(players)
-
-    near = lax.ppermute(embeddings, "dev", near_pairs)
-    far = lax.ppermute(embeddings, "dev", far_pairs)
+    z_near, z_swap, x_near, x_swap = plan(players)
+
+    near = lax.ppermute(embeddings, "dev", z_near)
+    far = lax.ppermute(embeddings, "dev", z_swap)
+    x_first = lax.ppermute(embeddings, "dev", x_near)
+    x_second = lax.ppermute(embeddings, "dev", x_swap)
     normed, density = call(own_kernel, [embeddings], [block, sums], flops=tile)
-    density, to_near, near = call(
-        near_kernel, [normed, near, density], [sums, sums, block], flops=tile
-    )
-    to_near, to_far = call(
-        far_kernel, [near, far, to_near], [sums, sums], [block], flops=tile
-    )
-    from_near = lax.ppermute(to_near, "dev", inverse(near_pairs))
-    from_far = lax.ppermute(to_far, "dev", inverse(far_pairs))
-    weights, total = call(
-        weight_kernel, [density, from_near, from_far], [sums, ((players, LANES), f32)]
-    )
+
+    density, to_near, to_far = call(
+        x_kernel,
+        [normed, x_first, x_second, density],
+        [sums, sums, sums],
+        [block, block],
+        flops=2 * tile,
+    )
+    from_near = lax.ppermute(to_near, "dev", inverse(x_near))
+    from_far = lax.ppermute(to_far, "dev", inverse(x_swap))
+    (density,) = call(add_kernel, [density, from_near, from_far], [sums])
+    part = lax.ppermute(density, "dev", z_near)
+
+    (near,) = call(near_kernel, [near, part], [block])
+    part, to_far = call(far_kernel, [near, far, part], [sums, sums], [block], flops=tile)
+    from_far = lax.ppermute(to_far, "dev", z_swap)
+    density, part = call(
+        own_near_kernel, [normed, near, density, part], [sums, sums], flops=tile
+    )
+    weights, near_weights, total = call(
+        weight_kernel,
+        [density, part, from_far],
+        [sums, sums, ((players, LANES), f32)],
+    )
+    sent_weights = lax.ppermute(near_weights, "dev", inverse(z_near))
     totals = lax.all_to_all(total, "dev", 0, 0, tiled=True)
     (keep,) = call(
-        functools.partial(scale_kernel, rows=float(players * rows)), [weights, totals], [sums]
+        functools.partial(scale_kernel, rows=float(players * rows)),
+        [weights, sent_weights, totals],
+        [sums],
     )
     return keep.reshape(rows)
 

time: 78 us -> 86.1 us (1.10)
  starting transfers between devices: 12.1 us -> 40.3 us
  blocking collectives: 27.1 us -> 0 us
  waiting for transfers between devices: 29.4 us -> 35.4 us
    all_to_all x1 -> x0, blocking collectives: 27.1 us -> none  [shards(): totals = lax.all_to_all(total, 'dev', 0, 0, tiled=True)]
    ppermute x4 -> x9, starting transfers between devices: 12.1 us -> 27.6 us  [the longest x1 7.93 us: shards(): far = lax.ppermute(embeddings, 'dev', z_swap)]
    all_to_all x0 -> x1, starting transfers between devices: none -> 12.7 us  [shards(): totals = lax.all_to_all(total, 'dev', 0, 0, tiled=True)]
    all_to_all x0 -> x1, waiting for transfers between devices: none -> 7.53 us  [shards(): totals = lax.all_to_all(total, 'dev', 0, 0, tiled=True)]
    ppermute x4 -> x9, waiting for transfers between devices: 29.4 us -> 27.8 us  [the longest x1 13.1 us: shards(): near = lax.ppermute(embeddings, 'dev', z_near)]
    pallas_call x5 -> x8, Pallas kernels: 7.79 us -> 8.59 us  [call(): pl.pallas_call(kernel, out_shape=shapes, in_specs=[space] * len(operands)...]
  transfers between devices with their start and end apart: 4 -> 10, of which waited for: 3 -> 6; matrix products, arithmetic and copies ran while one was open for 0% -> 0% of each run, Pallas kernels for 6% -> 6%
where the time goes in v5:
time: 86.1 us; the launch traced here: 85.8 us
  starting transfers between devices  40.3 us (47%)
  waiting for transfers between devices  35.4 us (41%)
  Pallas kernels  8.59 us (10%)
  local copies, waits for them, and re-layouts  1.41 us (2%)
    ppermute x1, waiting for transfers between devices, shards(): near = lax.ppermute(embeddings, 'dev', z_near)  13.1 us
    all_to_all x1, starting transfers between devices, shards(): totals = lax.all_to_all(total, 'dev', 0, 0, tiled=True)  12.7 us
    pallas_call x8, Pallas kernels, call(): pl.pallas_call(kernel, out_shape=shapes, in_specs=[space] * len(operands)...  8.59 us
    ppermute x1, waiting for transfers between devices, shards(): from_near = lax.ppermute(to_near, 'dev', inverse(x_near))  7.99 us
    ppermute x1, starting transfers between devices, shards(): far = lax.ppermute(embeddings, 'dev', z_swap)  7.93 us
    all_to_all x1, waiting for transfers between devices, shards(): totals = lax.all_to_all(total, 'dev', 0, 0, tiled=True)  7.53 us
    ppermute x1, starting transfers between devices, shards(): from_far = lax.ppermute(to_far, 'dev', z_swap)  5.79 us
    ppermute x1, starting transfers between devices, shards(): sent_weights = lax.ppermute(near_weights, 'dev', inverse(z_near))  4.58 us
  transfers between devices with their start and end apart: 10, of which 6 were waited for; matrix products, arithmetic and copies ran while one was open for 0% of the time, Pallas kernels for 6%

profile of v5, /device:TPU:1, one launch (start us, length us, event | category | flops | bytes accessed | tf_op | source)
XLA Modules:
  0.0 85.8 jit_solution(1141259217051415650)
XLA Ops:
  0.0 4.0 %collective-permute-start.1 = (bf16[1024,768]{1,0:T(8,128)(2,1)}, bf16[1024,768]{1,0:T(8,128)(2,1)S(1)}, u32[]{:S(2)}, u32[]{:S(2)}) collective-permute-start(bf16[1024,768]{1,0:T(8,128)(2,1)} %raw.1), channel_id=1, source_target_pairs={{1,65},{3,67},{5,69},{7,71},{9,73},{11,75},{13,77},{15,79},{16,80}... | collective-permute-start | bytes 4718600 | tf_op jit(solution)/shard_map/ppermute | solution.py:187
  4.0 0.8 collective-permute-start.2
  4.8 1.3 %collective-permute-start = (bf16[1024,768]{1,0:T(8,128)(2,1)}, bf16[1024,768]{1,0:T(8,128)(2,1)S(1)}, u32[]{:S(2)}, u32[]{:S(2)}) collective-permute-start(bf16[1024,768]{1,0:T(8,128)(2,1)} %raw.1), channel_id=1, source_target_pairs={{0,16},{2,18},{4,20},{6,22},{8,24},{10,26},{12,28},{14,30},{17,1},... | collective-permute-start | bytes 4718600 | tf_op jit(solution)/shard_map/ppermute | solution.py:185
  6.1 7.9 %collective-permute-start.6 = (bf16[1024,768]{1,0:T(8,128)(2,1)}, bf16[1024,768]{1,0:T(8,128)(2,1)S(1)}, u32[]{:S(2)}, u32[]{:S(2)}) collective-permute-start(bf16[1024,768]{1,0:T(8,128)(2,1)} %raw.1), channel_id=1, source_target_pairs={{1,49},{3,51},{5,53},{7,55},{9,57},{11,59},{13,61},{15,63},{16,32}... | collective-permute-start | bytes 4718600 | tf_op jit(solution)/shard_map/ppermute | solution.py:186
  14.0 0.0 copy-start
  14.1 1.4 %copy-done = bf16[1024,768]{1,0:T(8,128)(2,1)S(1)} copy-done((bf16[1024,768]{1,0:T(8,128)(2,1)S(1)}, bf16[1024,768]{1,0:T(8,128)(2,1)}, u32[]{:S(2)}) %copy-start) | copy-done | bytes 1572888
  15.5 2.3 %shard_map.17 = (bf16[1024,768]{1,0:T(8,128)(2,1)S(1)}, f32[8,128]{1,0:T(8,128)S(1)}) custom-call(bf16[1024,768]{1,0:T(8,128)(2,1)S(1)} %copy-done), custom_call_target="tpu_custom_call" | custom-call | flops 1610612736 | bytes 3149824 | tf_op jit(solution)/shard_map/pallas_call | solution.py:164
  17.8 3.8 %collective-permute-done.1.near_raw = bf16[1024,768]{1,0:T(8,128)(2,1)S(1)} collective-permute-done((bf16[1024,768]{1,0:T(8,128)(2,1)}, bf16[1024,768]{1,0:T(8,128)(2,1)S(1)}, u32[]{:S(2)}, u32[]{:S(2)}) %collective-permute-start.1) | collective-permute-done | bytes 1572896 | tf_op jit(solution)/shard_map/ppermute | solution.py:187
  21.6 0.0 collective-permute-done.2.far_raw
  21.6 1.3 %collective-permute-start.3 = (f32[8,128]{1,0:T(8,128)S(1)}, f32[8,128]{1,0:T(8,128)S(1)}, u32[]{:S(2)}, u32[]{:S(2)}) collective-permute-start(f32[8,128]{1,0:T(8,128)S(1)} %get-tuple-element.20), channel_id=1, source_target_pairs={{65,1},{67,3},{69,5},{71,7},{73,9},{75,11},{77,13},{79,15},{80,16}... | collective-permute-start | bytes 12296 | tf_op jit(solution)/shard_map/ppermute | solution.py:198
  22.9 0.7 collective-permute-start.4
  23.6 8.0 %collective-permute-done.3.second = f32[8,128]{1,0:T(8,128)S(1)} collective-permute-done((f32[8,128]{1,0:T(8,128)S(1)}, f32[8,128]{1,0:T(8,128)S(1)}, u32[]{:S(2)}, u32[]{:S(2)}) %collective-permute-start.3) | collective-permute-done | bytes 4128 | tf_op jit(solution)/shard_map/ppermute | solution.py:198
  31.6 0.0 collective-permute-done.4.third
  31.6 1.3 %collective-permute-start.5 = (f32[8,128]{1,0:T(8,128)S(1)}, f32[8,128]{1,0:T(8,128)S(1)}, u32[]{:S(2)}, u32[]{:S(2)}) collective-permute-start(f32[8,128]{1,0:T(8,128)S(1)} %shard_map.19.density), channel_id=1, source_target_pairs={{0,16},{2,18},{4,20},{6,22},{8,24},{10,26},{12,28},{14,30},{17,1},... | collective-permute-start | bytes 12296 | tf_op jit(solution)/shard_map/ppermute | solution.py:201
  32.9 13.1 %collective-permute-done.raw = bf16[1024,768]{1,0:T(8,128)(2,1)S(1)} collective-permute-done((bf16[1024,768]{1,0:T(8,128)(2,1)}, bf16[1024,768]{1,0:T(8,128)(2,1)S(1)}, u32[]{:S(2)}, u32[]{:S(2)}) %collective-permute-start) | collective-permute-done | bytes 1572896 | tf_op jit(solution)/shard_map/ppermute | solution.py:185
  46.0 0.0 collective-permute-done.5.part
  46.0 0.5 shard_map.20.near
  46.5 2.1 %collective-permute-done.6.raw = bf16[1024,768]{1,0:T(8,128)(2,1)S(1)} collective-permute-done((bf16[1024,768]{1,0:T(8,128)(2,1)}, bf16[1024,768]{1,0:T(8,128)(2,1)S(1)}, u32[]{:S(2)}, u32[]{:S(2)}) %collective-permute-start.6) | collective-permute-done | bytes 1572896 | tf_op jit(solution)/shard_map/ppermute | solution.py:186
  48.6 2.3 %shard_map.21 = (f32[8,128]{1,0:T(8,128)S(1)}, f32[8,128]{1,0:T(8,128)S(1)}) custom-call(bf16[1024,768]{1,0:T(8,128)(2,1)S(1)} %shard_map.20.near, bf16[1024,768]{1,0:T(8,128)(2,1)S(1)} %collective-permute-done.6.raw, f32[8,128]{1,0:T(8,128)S(1)} %collective-permute-done.5.part), custom_call_target="tpu_custom_call" | custom-call | flops 1610612736 | bytes 3158016 | tf_op jit(solution)/shard_map/pallas_call | solution.py:164
  50.9 5.8 %collective-permute-start.7 = (f32[8,128]{1,0:T(8,128)S(1)}, f32[8,128]{1,0:T(8,128)S(1)}, u32[]{:S(2)}, u32[]{:S(2)}) collective-permute-start(f32[8,128]{1,0:T(8,128)S(1)} %get-tuple-element.25), channel_id=1, source_target_pairs={{1,49},{3,51},{5,53},{7,55},{9,57},{11,59},{13,61},{15,63},{16,32}... | collective-permute-start | bytes 12296 | tf_op jit(solution)/shard_map/ppermute | solution.py:205
  56.7 2.0 %shard_map.22 = (f32[8,128]{1,0:T(8,128)S(1)}, f32[8,128]{1,0:T(8,128)S(1)}) custom-call(bf16[1024,768]{1,0:T(8,128)(2,1)S(1)} %get-tuple-element.17.normed, bf16[1024,768]{1,0:T(8,128)(2,1)S(1)} %shard_map.20.near, f32[8,128]{1,0:T(8,128)S(1)} %shard_map.19.density, f32[8,128]{1,0:T(8,128)S(1)} %get-tuple-element.22.part), custom_call_target="tpu_custom_call" | custom-call | flops 1610612736 | bytes 3162112 | tf_op jit(solution)/shard_map/pallas_call | solution.py:164
  58.8 0.0 collective-permute-done.7.from_far
  58.8 0.8 shard_map.23
  59.6 12.7 %all-to-all-start = ((f32[256,1,128]{2,1,0:T(1,128)}), f32[256,1,128]{2,1,0:T(1,128)S(1)}, u32[]{:S(2)}, u32[]{:S(2)}) async-start(f32[256,1,128]{2,1,0:T(1,128)} %bitcast.1), calls=%async_computation | async-start | bytes 262144 | tf_op jit(solution)/shard_map/all_to_all | solution.py:215
  72.3 4.6 %collective-permute-start.8 = (f32[8,128]{1,0:T(8,128)S(1)}, f32[8,128]{1,0:T(8,128)S(1)}, u32[]{:S(2)}, u32[]{:S(2)}) collective-permute-start(f32[8,128]{1,0:T(8,128)S(1)} %get-tuple-element.27), channel_id=1, source_target_pairs={{16,0},{18,2},{20,4},{22,6},{24,8},{26,10},{28,12},{30,14},{1,17},... | collective-permute-start | bytes 12296 | tf_op jit(solution)/shard_map/ppermute | solution.py:214
  76.8 0.7 collective-permute-done.8.sent_weights
  77.6 7.5 %all-to-all-done = f32[256,1,128]{2,1,0:T(1,128)S(1)} async-done(((f32[256,1,128]{2,1,0:T(1,128)}), f32[256,1,128]{2,1,0:T(1,128)S(1)}, u32[]{:S(2)}, u32[]{:S(2)}) %all-to-all-start) | async-done | bytes 131104 | tf_op jit(solution)/shard_map/all_to_all | solution.py:215
  85.1 0.6 shard_map.24
  (2 shorter events, 0.0 us)
Async XLA Ops:
  0.0 21.6 %collective-permute-start.1 = (bf16[1024,768]{1,0:T(8,128)(2,1)}, bf16[1024,768]{1,0:T(8,128)(2,1)S(1)}, u32[]{:S(2)}, u32[]{:S(2)}) collective-permute-start(bf16[1024,768]{1,0:T(8,128)(2,1)} %raw.1), channel_id=1, source_target_pairs={{1,65},{3,67},{5,69},{7,71},{9,73},{11,75},{13,77},{15,79},{16,80}... | collective-permute-start | bytes 4718600 | tf_op jit(solution)/shard_map/ppermute | solution.py:187
  4.0 17.6 %collective-permute-start.2 = (bf16[1024,768]{1,0:T(8,128)(2,1)}, bf16[1024,768]{1,0:T(8,128)(2,1)S(1)}, u32[]{:S(2)}, u32[]{:S(2)}) collective-permute-start(bf16[1024,768]{1,0:T(8,128)(2,1)} %raw.1), channel_id=1, source_target_pairs={{0,192},{2,194},{4,196},{6,198},{8,200},{10,202},{12,204},{14,206}... | collective-permute-start | bytes 4718600 | tf_op jit(solution)/shard_map/ppermute | solution.py:188
  4.8 41.2 %collective-permute-start = (bf16[1024,768]{1,0:T(8,128)(2,1)}, bf16[1024,768]{1,0:T(8,128)(2,1)S(1)}, u32[]{:S(2)}, u32[]{:S(2)}) collective-permute-start(bf16[1024,768]{1,0:T(8,128)(2,1)} %raw.1), channel_id=1, source_target_pairs={{0,16},{2,18},{4,20},{6,22},{8,24},{10,26},{12,28},{14,30},{17,1},... | collective-permute-start | bytes 4718600 | tf_op jit(solution)/shard_map/ppermute | solution.py:185
  6.1 42.5 %collective-permute-start.6 = (bf16[1024,768]{1,0:T(8,128)(2,1)}, bf16[1024,768]{1,0:T(8,128)(2,1)S(1)}, u32[]{:S(2)}, u32[]{:S(2)}) collective-permute-start(bf16[1024,768]{1,0:T(8,128)(2,1)} %raw.1), channel_id=1, source_target_pairs={{1,49},{3,51},{5,53},{7,55},{9,57},{11,59},{13,61},{15,63},{16,32}... | collective-permute-start | bytes 4718600 | tf_op jit(solution)/shard_map/ppermute | solution.py:186
  14.0 1.4 %copy-start = (bf16[1024,768]{1,0:T(8,128)(2,1)S(1)}, bf16[1024,768]{1,0:T(8,128)(2,1)}, u32[]{:S(2)}) copy-start(bf16[1024,768]{1,0:T(8,128)(2,1)} %raw.1) | copy-start | bytes 4718596
  21.6 10.0 %collective-permute-start.3 = (f32[8,128]{1,0:T(8,128)S(1)}, f32[8,128]{1,0:T(8,128)S(1)}, u32[]{:S(2)}, u32[]{:S(2)}) collective-permute-start(f32[8,128]{1,0:T(8,128)S(1)} %get-tuple-element.20), channel_id=1, source_target_pairs={{65,1},{67,3},{69,5},{71,7},{73,9},{75,11},{77,13},{79,15},{80,16}... | collective-permute-start | bytes 12296 | tf_op jit(solution)/shard_map/ppermute | solution.py:198
  22.9 8.7 %collective-permute-start.4 = (f32[8,128]{1,0:T(8,128)S(1)}, f32[8,128]{1,0:T(8,128)S(1)}, u32[]{:S(2)}, u32[]{:S(2)}) collective-permute-start(f32[8,128]{1,0:T(8,128)S(1)} %get-tuple-element.21), channel_id=1, source_target_pairs={{192,0},{194,2},{196,4},{198,6},{200,8},{202,10},{204,12},{206,14}... | collective-permute-start | bytes 12296 | tf_op jit(solution)/shard_map/ppermute | solution.py:199
  31.6 14.4 %collective-permute-start.5 = (f32[8,128]{1,0:T(8,128)S(1)}, f32[8,128]{1,0:T(8,128)S(1)}, u32[]{:S(2)}, u32[]{:S(2)}) collective-permute-start(f32[8,128]{1,0:T(8,128)S(1)} %shard_map.19.density), channel_id=1, source_target_pairs={{0,16},{2,18},{4,20},{6,22},{8,24},{10,26},{12,28},{14,30},{17,1},... | collective-permute-start | bytes 12296 | tf_op jit(solution)/shard_map/ppermute | solution.py:201
  50.9 7.8 %collective-permute-start.7 = (f32[8,128]{1,0:T(8,128)S(1)}, f32[8,128]{1,0:T(8,128)S(1)}, u32[]{:S(2)}, u32[]{:S(2)}) collective-permute-start(f32[8,128]{1,0:T(8,128)S(1)} %get-tuple-element.25), channel_id=1, source_target_pairs={{1,49},{3,51},{5,53},{7,55},{9,57},{11,59},{13,61},{15,63},{16,32}... | collective-permute-start | bytes 12296 | tf_op jit(solution)/shard_map/ppermute | solution.py:205
  59.6 25.5 %all-to-all-start = ((f32[256,1,128]{2,1,0:T(1,128)}), f32[256,1,128]{2,1,0:T(1,128)S(1)}, u32[]{:S(2)}, u32[]{:S(2)}) async-start(f32[256,1,128]{2,1,0:T(1,128)} %bitcast.1), calls=%async_computation | async-start | bytes 262144 | tf_op jit(solution)/shard_map/all_to_all | solution.py:215
  72.3 5.3 %collective-permute-start.8 = (f32[8,128]{1,0:T(8,128)S(1)}, f32[8,128]{1,0:T(8,128)S(1)}, u32[]{:S(2)}, u32[]{:S(2)}) collective-permute-start(f32[8,128]{1,0:T(8,128)S(1)} %get-tuple-element.27), channel_id=1, source_target_pairs={{16,0},{18,2},{20,4},{22,6},{24,8},{26,10},{28,12},{30,14},{1,17},... | collective-permute-start | bytes 12296 | tf_op jit(solution)/shard_map/ppermute | solution.py:214

commit v6 on v4

--- a/solution.py
+++ b/solution.py
@@ -88,16 +88,19 @@
     tile_sums(normed, normed, density, 0, False, None, 0, False)
 
 
-def near_kernel(normed, raw, density, density_out, to_near, near):
-    unit_rows(raw, near)
-    density_out[...] = density[...]
-    tile_sums(normed, near, density_out, 0, True, to_near, 0, False)
+def unit_kernel(raw, normed):
+    unit_rows(raw, normed)
 
 
-def far_kernel(near, raw, to_near, near_out, to_far, far):
-    unit_rows(raw, far)
+def pair_kernel(raw, far, near, to_near, to_far):
+    unit_rows(raw, near)
+    tile_sums(near, far, to_near, 0, False, to_far, 0, False)
+
+
+def near_kernel(normed, near, density, to_near, density_out, near_out):
+    density_out[...] = density[...]
     near_out[...] = to_near[...]
-    tile_sums(near, far, near_out, 0, True, to_far, 0, False)
+    tile_sums(normed, near, density_out, 0, True, near_out, 0, True)
 
 
 def weight_kernel(density, from_near, from_far, weights, total):
@@ -139,14 +142,13 @@
     near = lax.ppermute(embeddings, "dev", near_pairs)
     far = lax.ppermute(embeddings, "dev", far_pairs)
     normed, density = call(own_kernel, [embeddings], [block, sums], flops=tile)
-    density, to_near, near = call(
-        near_kernel, [normed, near, density], [sums, sums, block], flops=tile
-    )
-    to_near, to_far = call(
-        far_kernel, [near, far, to_near], [sums, sums], [block], flops=tile
+    (far,) = call(unit_kernel, [far], [block])
+    near, to_near, to_far = call(pair_kernel, [near, far], [block, sums, sums], flops=tile)
+    from_far = lax.ppermute(to_far, "dev", inverse(far_pairs))
+    density, to_near = call(
+        near_kernel, [normed, near, density, to_near], [sums, sums], flops=tile
     )
     from_near = lax.ppermute(to_near, "dev", inverse(near_pairs))
-    from_far = lax.ppermute(to_far, "dev", inverse(far_pairs))
     weights, total = call(
         weight_kernel, [density, from_near, from_far], [sums, ((players, LANES), f32)]
     )

time: 78 us -> 79 us (1.013)
  waiting for transfers between devices: 29.4 us -> 35.6 us
  starting transfers between devices: 12.1 us -> 8.88 us
  blocking collectives: 27.1 us -> 24.9 us
    ppermute x1, waiting for transfers between devices: 1.32 us -> 30.8 us  [shards(): far = lax.ppermute(embeddings, 'dev', far_pairs)]
    ppermute x1, waiting for transfers between devices: 27.1 us -> 2.14 us  [shards(): near = lax.ppermute(embeddings, 'dev', near_pairs)]
    all_to_all x1, blocking collectives: 27.1 us -> 24.9 us  [shards(): totals = lax.all_to_all(total, 'dev', 0, 0, tiled=True)]
    ppermute x1, starting transfers between devices: 2.04 us -> 0.01 us  [shards(): near = lax.ppermute(embeddings, 'dev', near_pairs)]
    ppermute x1, starting transfers between devices: 3.96 us -> 1.94 us  [shards(): from_far = lax.ppermute(to_far, 'dev', inverse(far_pairs))]
    ppermute x1, waiting for transfers between devices: 0.99 us -> 2.21 us  [shards(): from_far = lax.ppermute(to_far, 'dev', inverse(far_pairs))]
    ppermute x1, starting transfers between devices: 6.02 us -> 6.85 us  [shards(): far = lax.ppermute(embeddings, 'dev', far_pairs)]
    pallas_call x5 -> x6, Pallas kernels: 7.79 us -> 7.92 us  [call(): pl.pallas_call(kernel, out_shape=shapes, in_specs=[space] * len(operands)...]
  transfers between devices with their start and end apart: 4 -> 4, of which waited for: 3 -> 4; matrix products, arithmetic and copies ran while one was open for 0% -> 0% of each run, Pallas kernels for 6% -> 4%
where the time goes in v6:
time: 79 us; the launch traced here: 78.8 us
  waiting for transfers between devices  35.6 us (45%)
  blocking collectives  24.9 us (32%)
  starting transfers between devices  8.88 us (11%)
  Pallas kernels  7.92 us (10%)
  local copies, waits for them, and re-layouts  1.47 us (2%)
    ppermute x1, waiting for transfers between devices, shards(): far = lax.ppermute(embeddings, 'dev', far_pairs)  30.8 us
    all_to_all x1, blocking collectives, shards(): totals = lax.all_to_all(total, 'dev', 0, 0, tiled=True)  24.9 us
    pallas_call x6, Pallas kernels, call(): pl.pallas_call(kernel, out_shape=shapes, in_specs=[space] * len(operands)...  7.92 us
    ppermute x1, starting transfers between devices, shards(): far = lax.ppermute(embeddings, 'dev', far_pairs)  6.85 us
    ppermute x1, waiting for transfers between devices, shards(): from_far = lax.ppermute(to_far, 'dev', inverse(far_pairs))  2.21 us
    ppermute x1, waiting for transfers between devices, shards(): near = lax.ppermute(embeddings, 'dev', near_pairs)  2.14 us
    ppermute x1, starting transfers between devices, shards(): from_far = lax.ppermute(to_far, 'dev', inverse(far_pairs))  1.94 us
  transfers between devices with their start and end apart: 4, of which 4 were waited for; matrix products, arithmetic and copies ran while one was open for 0% of the time, Pallas kernels for 4%

profile of v6, /device:TPU:1, one launch (start us, length us, event | category | flops | bytes accessed | tf_op | source)
XLA Modules:
  0.0 78.8 jit_solution(5981271567549491600)
XLA Ops:
  0.0 6.8 %collective-permute-start.1 = (bf16[1024,768]{1,0:T(8,128)(2,1)}, bf16[1024,768]{1,0:T(8,128)(2,1)S(1)}, u32[]{:S(2)}, u32[]{:S(2)}) collective-permute-start(bf16[1024,768]{1,0:T(8,128)(2,1)} %raw.1), channel_id=1, source_target_pairs={{0,192},{1,49},{2,194},{3,51},{4,196},{5,53},{6,198},{7,55},{8,200... | collective-permute-start | bytes 4718600 | tf_op jit(solution)/shard_map/ppermute | solution.py:143
  6.9 0.0 collective-permute-start
  6.9 0.0 copy-start
  6.9 1.5 %copy-done = bf16[1024,768]{1,0:T(8,128)(2,1)S(1)} copy-done((bf16[1024,768]{1,0:T(8,128)(2,1)S(1)}, bf16[1024,768]{1,0:T(8,128)(2,1)}, u32[]{:S(2)}) %copy-start) | copy-done | bytes 1572888
  8.3 2.3 %shard_map.17 = (bf16[1024,768]{1,0:T(8,128)(2,1)S(1)}, f32[8,128]{1,0:T(8,128)S(1)}) custom-call(bf16[1024,768]{1,0:T(8,128)(2,1)S(1)} %copy-done), custom_call_target="tpu_custom_call" | custom-call | flops 1610612736 | bytes 3149824 | tf_op jit(solution)/shard_map/pallas_call | solution.py:121
  10.6 30.8 %collective-permute-done.1.raw = bf16[1024,768]{1,0:T(8,128)(2,1)S(1)} collective-permute-done((bf16[1024,768]{1,0:T(8,128)(2,1)}, bf16[1024,768]{1,0:T(8,128)(2,1)S(1)}, u32[]{:S(2)}, u32[]{:S(2)}) %collective-permute-start.1) | collective-permute-done | bytes 1572896 | tf_op jit(solution)/shard_map/ppermute | solution.py:143
  41.4 0.5 shard_map.18.far
  41.9 2.1 %collective-permute-done.raw = bf16[1024,768]{1,0:T(8,128)(2,1)S(1)} collective-permute-done((bf16[1024,768]{1,0:T(8,128)(2,1)}, bf16[1024,768]{1,0:T(8,128)(2,1)S(1)}, u32[]{:S(2)}, u32[]{:S(2)}) %collective-permute-start) | collective-permute-done | bytes 1572896 | tf_op jit(solution)/shard_map/ppermute | solution.py:142
  44.1 2.3 %shard_map.19 = (bf16[1024,768]{1,0:T(8,128)(2,1)S(1)}, f32[8,128]{1,0:T(8,128)S(1)}, f32[8,128]{1,0:T(8,128)S(1)}) custom-call(bf16[1024,768]{1,0:T(8,128)(2,1)S(1)} %collective-permute-done.raw, bf16[1024,768]{1,0:T(8,128)(2,1)S(1)} %shard_map.18.far), custom_call_target="tpu_custom_call" | custom-call | flops 1610612736 | bytes 4726784 | tf_op jit(solution)/shard_map/pallas_call | solution.py:121
  46.4 2.0 %shard_map.20 = (f32[8,128]{1,0:T(8,128)S(1)}, f32[8,128]{1,0:T(8,128)S(1)}) custom-call(bf16[1024,768]{1,0:T(8,128)(2,1)S(1)} %get-tuple-element.14.normed, bf16[1024,768]{1,0:T(8,128)(2,1)S(1)} %get-tuple-element.15.near, f32[8,128]{1,0:T(8,128)S(1)} %get-tuple-element.16.density, f32[8,128]{1,0:T(8,128)S(1)} %get-tuple-element.17.to_near), custom_call_target="tpu_custom_call" | custom-call | flops 1610612736 | bytes 3162112 | tf_op jit(solution)/shard_map/pallas_call | solution.py:121
  48.4 0.1 collective-permute-start.2
  48.5 1.9 %collective-permute-start.3 = (f32[8,128]{1,0:T(8,128)S(1)}, f32[8,128]{1,0:T(8,128)S(1)}, u32[]{:S(2)}, u32[]{:S(2)}) collective-permute-start(f32[8,128]{1,0:T(8,128)S(1)} %get-tuple-element.20), channel_id=1, source_target_pairs={{192,0},{49,1},{194,2},{51,3},{196,4},{53,5},{198,6},{55,7},{200,8... | collective-permute-start | bytes 12296 | tf_op jit(solution)/shard_map/ppermute | solution.py:147
  50.4 0.5 collective-permute-done.2.from_near
  50.9 2.2 %collective-permute-done.3.from_far = f32[8,128]{1,0:T(8,128)S(1)} collective-permute-done((f32[8,128]{1,0:T(8,128)S(1)}, f32[8,128]{1,0:T(8,128)S(1)}, u32[]{:S(2)}, u32[]{:S(2)}) %collective-permute-start.3) | collective-permute-done | bytes 4128 | tf_op jit(solution)/shard_map/ppermute | solution.py:147
  53.1 0.1 shard_map.21
  53.3 24.9 %all_to_all.11 = f32[256,1,128]{2,1,0:T(1,128)S(1)} all-to-all(f32[256,1,128]{2,1,0:T(1,128)S(1)} %bitcast.6), channel_id=1, replica_groups=mesh['dev'=256] {'dev'}, dimensions={0} | all-to-all | bytes 262144 | tf_op jit(solution)/shard_map/all_to_all | solution.py:155
  78.2 0.6 shard_map.22
Async XLA Ops:
  0.0 41.4 %collective-permute-start.1 = (bf16[1024,768]{1,0:T(8,128)(2,1)}, bf16[1024,768]{1,0:T(8,128)(2,1)S(1)}, u32[]{:S(2)}, u32[]{:S(2)}) collective-permute-start(bf16[1024,768]{1,0:T(8,128)(2,1)} %raw.1), channel_id=1, source_target_pairs={{0,192},{1,49},{2,194},{3,51},{4,196},{5,53},{6,198},{7,55},{8,200... | collective-permute-start | bytes 4718600 | tf_op jit(solution)/shard_map/ppermute | solution.py:143
  6.9 37.2 %collective-permute-start = (bf16[1024,768]{1,0:T(8,128)(2,1)}, bf16[1024,768]{1,0:T(8,128)(2,1)S(1)}, u32[]{:S(2)}, u32[]{:S(2)}) collective-permute-start(bf16[1024,768]{1,0:T(8,128)(2,1)} %raw.1), channel_id=1, source_target_pairs={{0,16},{1,65},{2,18},{3,67},{4,20},{5,69},{6,22},{7,71},{8,24},{9,... | collective-permute-start | bytes 4718600 | tf_op jit(solution)/shard_map/ppermute | solution.py:142
  6.9 1.5 %copy-start = (bf16[1024,768]{1,0:T(8,128)(2,1)S(1)}, bf16[1024,768]{1,0:T(8,128)(2,1)}, u32[]{:S(2)}) copy-start(bf16[1024,768]{1,0:T(8,128)(2,1)} %raw.1) | copy-start | bytes 4718596
  48.4 2.5 %collective-permute-start.2 = (f32[8,128]{1,0:T(8,128)S(1)}, f32[8,128]{1,0:T(8,128)S(1)}, u32[]{:S(2)}, u32[]{:S(2)}) collective-permute-start(f32[8,128]{1,0:T(8,128)S(1)} %get-tuple-element.19), channel_id=1, source_target_pairs={{16,0},{65,1},{18,2},{67,3},{20,4},{69,5},{22,6},{71,7},{24,8},{73... | collective-permute-start | bytes 12296 | tf_op jit(solution)/shard_map/ppermute | solution.py:151
  48.5 4.7 %collective-permute-start.3 = (f32[8,128]{1,0:T(8,128)S(1)}, f32[8,128]{1,0:T(8,128)S(1)}, u32[]{:S(2)}, u32[]{:S(2)}) collective-permute-start(f32[8,128]{1,0:T(8,128)S(1)} %get-tuple-element.20), channel_id=1, source_target_pairs={{192,0},{49,1},{194,2},{51,3},{196,4},{53,5},{198,6},{55,7},{200,8... | collective-permute-start | bytes 12296 | tf_op jit(solution)/shard_map/ppermute | solution.py:147

commit v7 on v6

--- a/solution.py
+++ b/solution.py
@@ -103,8 +103,12 @@
     tile_sums(normed, near, density_out, 0, True, near_out, 0, True)
 
 
-def weight_kernel(density, from_near, from_far, weights, total):
-    value = 1.0 / (density[...] + from_near[...] + from_far[...])
+def add_kernel(density, from_far, out):
+    out[...] = density[...] + from_far[...]
+
+
+def weight_kernel(density, from_near, weights, total):
+    value = 1.0 / (density[...] + from_near[...])
     weights[...] = value
     total[...] = jnp.full(total.shape, jnp.sum(value))
 
@@ -149,8 +153,9 @@
         near_kernel, [normed, near, density, to_near], [sums, sums], flops=tile
     )
     from_near = lax.ppermute(to_near, "dev", inverse(near_pairs))
+    (density,) = call(add_kernel, [density, from_far], [sums])
     weights, total = call(
-        weight_kernel, [density, from_near, from_far], [sums, ((players, LANES), f32)]
+        weight_kernel, [density, from_near], [sums, ((players, LANES), f32)]
     )
     totals = lax.all_to_all(total, "dev", 0, 0, tiled=True)
     (keep,) = call(

time: 79 us -> 79.3 us (level)
  waiting for transfers between devices: 35.6 us -> 34.8 us
    ppermute x1, waiting for transfers between devices: 2.21 us -> 0.08 us  [shards(): from_far = lax.ppermute(to_far, 'dev', inverse(far_pairs))]
    ppermute x1, waiting for transfers between devices: 0.5 us -> 1.83 us  [shards(): from_near = lax.ppermute(to_near, 'dev', inverse(near_pairs))]
    pallas_call x6 -> x7, Pallas kernels: 7.92 us -> 7.92 us  [call(): pl.pallas_call(kernel, out_shape=shapes, in_specs=[space] * len(operands)...]
  transfers between devices with their start and end apart: 4 -> 4, of which waited for: 4 -> 4; matrix products, arithmetic and copies ran while one was open for 0% -> 0% of each run, Pallas kernels for 4% -> 6%
where the time goes in v7:
time: 79.3 us; the launch traced here: 79.2 us
  waiting for transfers between devices  34.8 us (44%)
  blocking collectives  25.5 us (32%)
  starting transfers between devices  9.42 us (12%)
  Pallas kernels  7.92 us (10%)
  local copies, waits for them, and re-layouts  1.47 us (2%)
    ppermute x1, waiting for transfers between devices, shards(): far = lax.ppermute(embeddings, 'dev', far_pairs)  30.8 us
    all_to_all x1, blocking collectives, shards(): totals = lax.all_to_all(total, 'dev', 0, 0, tiled=True)  25.5 us
    pallas_call x7, Pallas kernels, call(): pl.pallas_call(kernel, out_shape=shapes, in_specs=[space] * len(operands)...  7.92 us
    ppermute x1, starting transfers between devices, shards(): far = lax.ppermute(embeddings, 'dev', far_pairs)  6.85 us
    ppermute x1, waiting for transfers between devices, shards(): near = lax.ppermute(embeddings, 'dev', near_pairs)  2.14 us
    ppermute x1, starting transfers between devices, shards(): from_far = lax.ppermute(to_far, 'dev', inverse(far_pairs))  1.94 us
    ppermute x1, waiting for transfers between devices, shards(): from_near = lax.ppermute(to_near, 'dev', inverse(near_pairs))  1.83 us
  transfers between devices with their start and end apart: 4, of which 4 were waited for; matrix products, arithmetic and copies ran while one was open for 0% of the time, Pallas kernels for 6%

profile of v7, /device:TPU:1, one launch (start us, length us, event | category | flops | bytes accessed | tf_op | source)
XLA Modules:
  0.0 79.2 jit_solution(11846723068079621014)
XLA Ops:
  0.0 6.8 %collective-permute-start.1 = (bf16[1024,768]{1,0:T(8,128)(2,1)}, bf16[1024,768]{1,0:T(8,128)(2,1)S(1)}, u32[]{:S(2)}, u32[]{:S(2)}) collective-permute-start(bf16[1024,768]{1,0:T(8,128)(2,1)} %raw.1), channel_id=1, source_target_pairs={{0,192},{1,49},{2,194},{3,51},{4,196},{5,53},{6,198},{7,55},{8,200... | collective-permute-start | bytes 4718600 | tf_op jit(solution)/shard_map/ppermute | solution.py:147
  6.9 0.0 collective-permute-start
  6.9 0.0 copy-start
  6.9 1.5 %copy-done = bf16[1024,768]{1,0:T(8,128)(2,1)S(1)} copy-done((bf16[1024,768]{1,0:T(8,128)(2,1)S(1)}, bf16[1024,768]{1,0:T(8,128)(2,1)}, u32[]{:S(2)}) %copy-start) | copy-done | bytes 1572888
  8.3 2.3 %shard_map.17 = (bf16[1024,768]{1,0:T(8,128)(2,1)S(1)}, f32[8,128]{1,0:T(8,128)S(1)}) custom-call(bf16[1024,768]{1,0:T(8,128)(2,1)S(1)} %copy-done), custom_call_target="tpu_custom_call" | custom-call | flops 1610612736 | bytes 3149824 | tf_op jit(solution)/shard_map/pallas_call | solution.py:125
  10.6 30.8 %collective-permute-done.1.raw = bf16[1024,768]{1,0:T(8,128)(2,1)S(1)} collective-permute-done((bf16[1024,768]{1,0:T(8,128)(2,1)}, bf16[1024,768]{1,0:T(8,128)(2,1)S(1)}, u32[]{:S(2)}, u32[]{:S(2)}) %collective-permute-start.1) | collective-permute-done | bytes 1572896 | tf_op jit(solution)/shard_map/ppermute | solution.py:147
  41.4 0.5 shard_map.18.far
  41.9 2.1 %collective-permute-done.raw = bf16[1024,768]{1,0:T(8,128)(2,1)S(1)} collective-permute-done((bf16[1024,768]{1,0:T(8,128)(2,1)}, bf16[1024,768]{1,0:T(8,128)(2,1)S(1)}, u32[]{:S(2)}, u32[]{:S(2)}) %collective-permute-start) | collective-permute-done | bytes 1572896 | tf_op jit(solution)/shard_map/ppermute | solution.py:146
  44.1 2.3 %shard_map.19 = (bf16[1024,768]{1,0:T(8,128)(2,1)S(1)}, f32[8,128]{1,0:T(8,128)S(1)}, f32[8,128]{1,0:T(8,128)S(1)}) custom-call(bf16[1024,768]{1,0:T(8,128)(2,1)S(1)} %collective-permute-done.raw, bf16[1024,768]{1,0:T(8,128)(2,1)S(1)} %shard_map.18.far), custom_call_target="tpu_custom_call" | custom-call | flops 1610612736 | bytes 4726784 | tf_op jit(solution)/shard_map/pallas_call | solution.py:125
  46.4 1.9 %collective-permute-start.2 = (f32[8,128]{1,0:T(8,128)S(1)}, f32[8,128]{1,0:T(8,128)S(1)}, u32[]{:S(2)}, u32[]{:S(2)}) collective-permute-start(f32[8,128]{1,0:T(8,128)S(1)} %get-tuple-element.19), channel_id=1, source_target_pairs={{192,0},{49,1},{194,2},{51,3},{196,4},{53,5},{198,6},{55,7},{200,8... | collective-permute-start | bytes 12296 | tf_op jit(solution)/shard_map/ppermute | solution.py:151
  48.3 2.0 %shard_map.20 = (f32[8,128]{1,0:T(8,128)S(1)}, f32[8,128]{1,0:T(8,128)S(1)}) custom-call(bf16[1024,768]{1,0:T(8,128)(2,1)S(1)} %get-tuple-element.14.normed, bf16[1024,768]{1,0:T(8,128)(2,1)S(1)} %get-tuple-element.15.near, f32[8,128]{1,0:T(8,128)S(1)} %get-tuple-element.16.density, f32[8,128]{1,0:T(8,128)S(1)} %get-tuple-element.17.to_near), custom_call_target="tpu_custom_call" | custom-call | flops 1610612736 | bytes 3162112 | tf_op jit(solution)/shard_map/pallas_call | solution.py:125
  50.3 0.6 collective-permute-start.3
  51.0 0.1 collective-permute-done.2.from_far
  51.0 1.8 %collective-permute-done.3.from_near = f32[8,128]{1,0:T(8,128)S(1)} collective-permute-done((f32[8,128]{1,0:T(8,128)S(1)}, f32[8,128]{1,0:T(8,128)S(1)}, u32[]{:S(2)}, u32[]{:S(2)}) %collective-permute-start.3) | collective-permute-done | bytes 4128 | tf_op jit(solution)/shard_map/ppermute | solution.py:155
  52.9 0.1 shard_map.22
  53.0 25.5 %all_to_all.11 = f32[256,1,128]{2,1,0:T(1,128)S(1)} all-to-all(f32[256,1,128]{2,1,0:T(1,128)S(1)} %bitcast.6), channel_id=1, replica_groups=mesh['dev'=256] {'dev'}, dimensions={0} | all-to-all | bytes 262144 | tf_op jit(solution)/shard_map/all_to_all | solution.py:160
  78.5 0.6 shard_map.23
  (1 shorter events, 0.0 us)
Async XLA Ops:
  0.0 41.4 %collective-permute-start.1 = (bf16[1024,768]{1,0:T(8,128)(2,1)}, bf16[1024,768]{1,0:T(8,128)(2,1)S(1)}, u32[]{:S(2)}, u32[]{:S(2)}) collective-permute-start(bf16[1024,768]{1,0:T(8,128)(2,1)} %raw.1), channel_id=1, source_target_pairs={{0,192},{1,49},{2,194},{3,51},{4,196},{5,53},{6,198},{7,55},{8,200... | collective-permute-start | bytes 4718600 | tf_op jit(solution)/shard_map/ppermute | solution.py:147
  6.9 37.2 %collective-permute-start = (bf16[1024,768]{1,0:T(8,128)(2,1)}, bf16[1024,768]{1,0:T(8,128)(2,1)S(1)}, u32[]{:S(2)}, u32[]{:S(2)}) collective-permute-start(bf16[1024,768]{1,0:T(8,128)(2,1)} %raw.1), channel_id=1, source_target_pairs={{0,16},{1,65},{2,18},{3,67},{4,20},{5,69},{6,22},{7,71},{8,24},{9,... | collective-permute-start | bytes 4718600 | tf_op jit(solution)/shard_map/ppermute | solution.py:146
  6.9 1.5 %copy-start = (bf16[1024,768]{1,0:T(8,128)(2,1)S(1)}, bf16[1024,768]{1,0:T(8,128)(2,1)}, u32[]{:S(2)}) copy-start(bf16[1024,768]{1,0:T(8,128)(2,1)} %raw.1) | copy-start | bytes 4718596
  46.4 4.7 %collective-permute-start.2 = (f32[8,128]{1,0:T(8,128)S(1)}, f32[8,128]{1,0:T(8,128)S(1)}, u32[]{:S(2)}, u32[]{:S(2)}) collective-permute-start(f32[8,128]{1,0:T(8,128)S(1)} %get-tuple-element.19), channel_id=1, source_target_pairs={{192,0},{49,1},{194,2},{51,3},{196,4},{53,5},{198,6},{55,7},{200,8... | collective-permute-start | bytes 12296 | tf_op jit(solution)/shard_map/ppermute | solution.py:151
  50.3 2.5 %collective-permute-start.3 = (f32[8,128]{1,0:T(8,128)S(1)}, f32[8,128]{1,0:T(8,128)S(1)}, u32[]{:S(2)}, u32[]{:S(2)}) collective-permute-start(f32[8,128]{1,0:T(8,128)S(1)} %get-tuple-element.20), channel_id=1, source_target_pairs={{16,0},{65,1},{18,2},{67,3},{20,4},{69,5},{22,6},{71,7},{24,8},{73... | collective-permute-start | bytes 12296 | tf_op jit(solution)/shard_map/ppermute | solution.py:155

commit v8 on v6

--- a/solution.py
+++ b/solution.py
@@ -11,6 +11,8 @@
 ROUNDS = 4
 LANES = 128
 STEP = 256
+FIRST = 768
+COPIES = 4
 
 sharpness = 10.0
 RATE = sharpness * math.log2(math.e)
@@ -83,8 +85,25 @@
         put(col_out, col_start, jnp.sum(total, axis=0, keepdims=True), col_add)
 
 
-def own_kernel(raw, normed, density):
-    unit_rows(raw, normed)
+def take_kernel(raw, taken, sems, *, start):
+    rows = taken.shape[0] // COPIES
+    copies = [
+        pltpu.make_async_copy(
+            raw.at[pl.ds(start + k * rows, rows), :],
+            taken.at[pl.ds(k * rows, rows), :],
+            sems.at[k],
+        )
+        for k in range(COPIES)
+    ]
+    for copy in copies:
+        copy.start()
+    for copy in copies:
+        copy.wait()
+
+
+def own_kernel(first, second, normed, density):
+    unit_rows(first, normed.at[pl.ds(0, FIRST), :])
+    unit_rows(second, normed.at[pl.ds(FIRST, second.shape[0]), :])
     tile_sums(normed, normed, density, 0, False, None, 0, False)
 
 
@@ -92,15 +111,27 @@
     unit_rows(raw, normed)
 
 
-def pair_kernel(raw, far, near, to_near, to_far):
-    unit_rows(raw, near)
+def first_pair_kernel(normed, near_raw, far, density, density_out, near, to_near, to_far):
+    unit_rows(near_raw, near)
+    density_out[...] = density[...]
     tile_sums(near, far, to_near, 0, False, to_far, 0, False)
-
-
-def near_kernel(normed, near, density, to_near, density_out, near_out):
+    tile_sums(normed, near, density_out, 0, True, to_near, 0, True)
+
+
+def second_pair_kernel(
+    normed, near_first, far_first, near_raw, far_raw, density, to_near, to_far,
+    density_out, near_out, far_out, near, far,
+):
+    unit_rows(near_raw, near)
+    unit_rows(far_raw, far)
     density_out[...] = density[...]
-    near_out[...] = to_near[...]
-    tile_sums(normed, near, density_out, 0, True, near_out, 0, True)
+    count = FIRST // LANES
+    near_out[pl.ds(0, count), :] = to_near[...]
+    far_out[pl.ds(0, count), :] = to_far[...]
+    tile_sums(normed, near, density_out, 0, True, near_out, FIRST, False)
+    tile_sums(near_first, far, near_out, 0, True, far_out, FIRST, False)
+    tile_sums(near, far_first, near_out, FIRST, True, far_out, 0, True)
+    tile_sums(near, far, near_out, FIRST, True, far_out, FIRST, True)
 
 
 def weight_kernel(density, from_near, from_far, weights, total):
@@ -114,21 +145,32 @@
     keep[...] = weights[...] * rows / total
 
 
-def call(kernel, operands, outs, scratch=(), flops=0):
-    space = pl.BlockSpec(memory_space=pltpu.VMEM)
+def call(kernel, operands, outs, scratch=(), flops=0, space=pltpu.VMEM, limit=32):
     shapes = [jax.ShapeDtypeStruct(*out) for out in outs]
     moved = sum(math.prod(s.shape) * s.dtype.itemsize for s in [*operands, *shapes])
     return pl.pallas_call(
         kernel,
         out_shape=shapes,
-        in_specs=[space] * len(operands),
-        out_specs=[space] * len(shapes),
-        scratch_shapes=[pltpu.VMEM(*s) for s in scratch],
+        in_specs=[pl.BlockSpec(memory_space=space)] * len(operands),
+        out_specs=[pl.BlockSpec(memory_space=pltpu.VMEM)] * len(shapes),
+        scratch_shapes=list(scratch),
         cost_estimate=pl.CostEstimate(
             flops=flops, bytes_accessed=moved, transcendentals=0
         ),
-        compiler_params=pltpu.CompilerParams(vmem_limit_bytes=32 * 2**20),
+        compiler_params=pltpu.CompilerParams(vmem_limit_bytes=limit * 2**20),
     )(*operands)
+
+
+def take(rows, start, out):
+    (taken,) = call(
+        functools.partial(take_kernel, start=start),
+        [rows],
+        [out],
+        [pltpu.SemaphoreType.DMA((COPIES,))],
+        space=pltpu.HBM,
+        limit=16,
+    )
+    return taken
 
 
 def shards(embeddings):
@@ -136,19 +178,35 @@
     rows, width = embeddings.shape
     bf16, f32 = jnp.bfloat16, jnp.float32
     block, sums = ((rows, width), bf16), ((rows // LANES, LANES), f32)
+    part, rest = ((FIRST, width), bf16), ((rows - FIRST, width), bf16)
+    part_sums = ((FIRST // LANES, LANES), f32)
     tile = 2 * rows * rows * width
     near_pairs, far_pairs = plan(players)
 
-    near = lax.ppermute(embeddings, "dev", near_pairs)
-    far = lax.ppermute(embeddings, "dev", far_pairs)
-    normed, density = call(own_kernel, [embeddings], [block, sums], flops=tile)
-    (far,) = call(unit_kernel, [far], [block])
-    near, to_near, to_far = call(pair_kernel, [near, far], [block, sums, sums], flops=tile)
+    first = take(embeddings, 0, part)
+    far_first = lax.ppermute(first, "dev", far_pairs)
+    near_first = lax.ppermute(first, "dev", near_pairs)
+    second = take(embeddings, FIRST, rest)
+    far_second = lax.ppermute(second, "dev", far_pairs)
+    near_second = lax.ppermute(second, "dev", near_pairs)
+    normed, density = call(own_kernel, [first, second], [block, sums], flops=tile)
+
+    (far_first,) = call(unit_kernel, [far_first], [part])
+    density, near_first, to_near, to_far = call(
+        first_pair_kernel,
+        [normed, near_first, far_first, density],
+        [sums, part, part_sums, part_sums],
+        flops=tile * 21 // 16,
+    )
+    density, to_near, to_far = call(
+        second_pair_kernel,
+        [normed, near_first, far_first, near_second, far_second, density, to_near, to_far],
+        [sums, sums, sums],
+        [pltpu.VMEM(*rest)] * 2,
+        flops=tile * 11 // 16,
+    )
+    from_near = lax.ppermute(to_near, "dev", inverse(near_pairs))
     from_far = lax.ppermute(to_far, "dev", inverse(far_pairs))
-    density, to_near = call(
-        near_kernel, [normed, near, density, to_near], [sums, sums], flops=tile
-    )
-    from_near = lax.ppermute(to_near, "dev", inverse(near_pairs))
     weights, total = call(
         weight_kernel, [density, from_near, from_far], [sums, ((players, LANES), f32)]
     )

time: 79 us -> 77.4 us (0.980)
  waiting for transfers between devices: 35.6 us -> 31.9 us
  starting transfers between devices: 8.88 us -> 11 us
    ppermute x2 -> x4, waiting for transfers between devices: 32.9 us -> 28.7 us  [the longest x1 24.6 us: shards(): far_first = lax.ppermute(first, 'dev', far_pairs)]
    ppermute x2 -> x4, starting transfers between devices: 6.85 us -> 9.52 us  [the longest x1 6.94 us: shards(): far_first = lax.ppermute(first, 'dev', far_pairs)]
    pallas_call x6 -> x8, Pallas kernels: 7.92 us -> 8.32 us  [call(): pl.pallas_call(kernel, out_shape=shapes, in_specs=[pl.BlockSpec(memory_sp...]
  transfers between devices with their start and end apart: 4 -> 6, of which waited for: 4 -> 5; matrix products, arithmetic and copies ran while one was open for 0% -> 0% of each run, Pallas kernels for 4% -> 7%
where the time goes in v8:
time: 77.4 us; the launch traced here: 77.2 us
  waiting for transfers between devices  31.9 us (41%)
  blocking collectives  24.5 us (32%)
  starting transfers between devices  11 us (14%)
  Pallas kernels  8.32 us (11%)
  local copies, waits for them, and re-layouts  1.41 us (2%)
    ppermute x1, waiting for transfers between devices, shards(): far_first = lax.ppermute(first, 'dev', far_pairs)  24.6 us
    all_to_all x1, blocking collectives, shards(): totals = lax.all_to_all(total, 'dev', 0, 0, tiled=True)  24.5 us
    pallas_call x8, Pallas kernels, call(): pl.pallas_call(kernel, out_shape=shapes, in_specs=[pl.BlockSpec(memory_sp...  8.32 us
    ppermute x1, starting transfers between devices, shards(): far_first = lax.ppermute(first, 'dev', far_pairs)  6.94 us
    ppermute x1, starting transfers between devices, shards(): near_second = lax.ppermute(second, 'dev', near_pairs)  2.45 us
    ppermute x1, waiting for transfers between devices, shards(): near_first = lax.ppermute(first, 'dev', near_pairs)  2.37 us
    ppermute x1, waiting for transfers between devices, shards(): from_far = lax.ppermute(to_far, 'dev', inverse(far_pairs))  2.21 us
    ppermute x1, waiting for transfers between devices, shards(): near_second = lax.ppermute(second, 'dev', near_pairs)  1.66 us
  transfers between devices with their start and end apart: 6, of which 5 were waited for; matrix products, arithmetic and copies ran while one was open for 0% of the time, Pallas kernels for 7%

profile of v8, /device:TPU:1, one launch (start us, length us, event | category | flops | bytes accessed | tf_op | source)
XLA Modules:
  0.0 77.2 jit_solution(4450797949362636067)
XLA Ops:
  0.0 0.0 copy-start
  0.0 1.4 %copy-done = bf16[1024,768]{1,0:T(8,128)(2,1)S(1)} copy-done((bf16[1024,768]{1,0:T(8,128)(2,1)S(1)}, bf16[1024,768]{1,0:T(8,128)(2,1)}, u32[]{:S(2)}) %copy-start) | copy-done | bytes 1572888
  1.4 0.3 shard_map.17.first
  1.7 6.9 %collective-permute-start.1 = (bf16[768,768]{1,0:T(8,128)(2,1)S(1)}, bf16[768,768]{1,0:T(8,128)(2,1)S(1)}, u32[]{:S(2)}, u32[]{:S(2)}) collective-permute-start(bf16[768,768]{1,0:T(8,128)(2,1)S(1)} %shard_map.17.first), channel_id=1, source_target_pairs={{0,192},{1,49},{2,194},{3,51},{4,196},{5,53},{6,198},{7,55},{8,200... | collective-permute-start | bytes 3538952 | tf_op jit(solution)/shard_map/ppermute | solution.py:187
  8.6 0.0 collective-permute-start
  8.6 0.5 shard_map.18.second
  9.2 2.4 %collective-permute-start.2 = (bf16[256,768]{1,0:T(8,128)(2,1)S(1)}, bf16[256,768]{1,0:T(8,128)(2,1)S(1)}, u32[]{:S(2)}, u32[]{:S(2)}) collective-permute-start(bf16[256,768]{1,0:T(8,128)(2,1)S(1)} %shard_map.18.second), channel_id=1, source_target_pairs={{0,16},{1,65},{2,18},{3,67},{4,20},{5,69},{6,22},{7,71},{8,24},{9,... | collective-permute-start | bytes 1179656 | tf_op jit(solution)/shard_map/ppermute | solution.py:191
  11.6 0.1 collective-permute-start.3
  11.8 2.3 %shard_map.19 = (bf16[1024,768]{1,0:T(8,128)(2,1)S(1)}, f32[8,128]{1,0:T(8,128)S(1)}) custom-call(bf16[768,768]{1,0:T(8,128)(2,1)S(1)} %shard_map.17.first, bf16[256,768]{1,0:T(8,128)(2,1)S(1)} %shard_map.18.second), custom_call_target="tpu_custom_call" | custom-call | flops 1610612736 | bytes 3149824 | tf_op jit(solution)/shard_map/pallas_call | solution.py:151
  14.0 24.6 %collective-permute-done.1.raw = bf16[768,768]{1,0:T(8,128)(2,1)S(1)} collective-permute-done((bf16[768,768]{1,0:T(8,128)(2,1)S(1)}, bf16[768,768]{1,0:T(8,128)(2,1)S(1)}, u32[]{:S(2)}, u32[]{:S(2)}) %collective-permute-start.1) | collective-permute-done | bytes 1179680 | tf_op jit(solution)/shard_map/ppermute | solution.py:187
  38.7 0.4 shard_map.20.far.far_first
  39.1 2.4 %collective-permute-done.near_raw = bf16[768,768]{1,0:T(8,128)(2,1)S(1)} collective-permute-done((bf16[768,768]{1,0:T(8,128)(2,1)S(1)}, bf16[768,768]{1,0:T(8,128)(2,1)S(1)}, u32[]{:S(2)}, u32[]{:S(2)}) %collective-permute-start) | collective-permute-done | bytes 1179680 | tf_op jit(solution)/shard_map/ppermute | solution.py:188
  41.4 2.5 %shard_map.21 = (f32[8,128]{1,0:T(8,128)S(1)}, bf16[768,768]{1,0:T(8,128)(2,1)S(1)}, f32[6,128]{1,0:T(8,128)S(1)}, f32[6,128]{1,0:T(8,128)S(1)}) custom-call(bf16[1024,768]{1,0:T(8,128)(2,1)S(1)} %get-tuple-element.16.normed, bf16[768,768]{1,0:T(8,128)(2,1)S(1)} %collective-permute-done.near_raw, bf16[768,768]{1,0:T(8,128)(2,1)S(1)} %shard_map.20.far.far_first, ...), custom_call_target="tpu_custom_call" | custom-call | flops 2113929216 | bytes 5126144 | tf_op jit(solution)/shard_map/pallas_call | solution.py:151
  44.0 1.7 %collective-permute-done.2.near_raw = bf16[256,768]{1,0:T(8,128)(2,1)S(1)} collective-permute-done((bf16[256,768]{1,0:T(8,128)(2,1)S(1)}, bf16[256,768]{1,0:T(8,128)(2,1)S(1)}, u32[]{:S(2)}, u32[]{:S(2)}) %collective-permute-start.2) | collective-permute-done | bytes 393248 | tf_op jit(solution)/shard_map/ppermute | solution.py:191
  45.7 0.0 collective-permute-done.3.far_raw
  45.7 1.5 %shard_map.22 = (f32[8,128]{1,0:T(8,128)S(1)}, f32[8,128]{1,0:T(8,128)S(1)}, f32[8,128]{1,0:T(8,128)S(1)}) custom-call(bf16[1024,768]{1,0:T(8,128)(2,1)S(1)} %get-tuple-element.16.normed, bf16[768,768]{1,0:T(8,128)(2,1)S(1)} %get-tuple-element.18.near_first, bf16[768,768]{1,0:T(8,128)(2,1)S(1)} %shard_map.20.far.far_first, ...), custom_call_target="tpu_custom_call" | custom-call | flops 1107296256 | bytes 4741120 | tf_op jit(solution)/shard_map/pallas_call | solution.py:151
  47.2 0.1 collective-permute-start.4
  47.3 1.4 %collective-permute-start.5 = (f32[8,128]{1,0:T(8,128)S(1)}, f32[8,128]{1,0:T(8,128)S(1)}, u32[]{:S(2)}, u32[]{:S(2)}) collective-permute-start(f32[8,128]{1,0:T(8,128)S(1)} %get-tuple-element.24), channel_id=1, source_target_pairs={{192,0},{49,1},{194,2},{51,3},{196,4},{53,5},{198,6},{55,7},{200,8... | collective-permute-start | bytes 12296 | tf_op jit(solution)/shard_map/ppermute | solution.py:209
  48.7 1.1 %collective-permute-done.4.from_near = f32[8,128]{1,0:T(8,128)S(1)} collective-permute-done((f32[8,128]{1,0:T(8,128)S(1)}, f32[8,128]{1,0:T(8,128)S(1)}, u32[]{:S(2)}, u32[]{:S(2)}) %collective-permute-start.4) | collective-permute-done | bytes 4128 | tf_op jit(solution)/shard_map/ppermute | solution.py:208
  49.7 2.2 %collective-permute-done.5.from_far = f32[8,128]{1,0:T(8,128)S(1)} collective-permute-done((f32[8,128]{1,0:T(8,128)S(1)}, f32[8,128]{1,0:T(8,128)S(1)}, u32[]{:S(2)}, u32[]{:S(2)}) %collective-permute-start.5) | collective-permute-done | bytes 4128 | tf_op jit(solution)/shard_map/ppermute | solution.py:209
  51.9 0.1 shard_map.23
  52.1 24.5 %all_to_all.11 = f32[256,1,128]{2,1,0:T(1,128)S(1)} all-to-all(f32[256,1,128]{2,1,0:T(1,128)S(1)} %bitcast.6), channel_id=1, replica_groups=mesh['dev'=256] {'dev'}, dimensions={0} | all-to-all | bytes 262144 | tf_op jit(solution)/shard_map/all_to_all | solution.py:213
  76.6 0.6 shard_map.24
Async XLA Ops:
  0.0 1.4 %copy-start = (bf16[1024,768]{1,0:T(8,128)(2,1)S(1)}, bf16[1024,768]{1,0:T(8,128)(2,1)}, u32[]{:S(2)}) copy-start(bf16[1024,768]{1,0:T(8,128)(2,1)} %raw.3) | copy-start | bytes 4718596
  1.7 37.0 %collective-permute-start.1 = (bf16[768,768]{1,0:T(8,128)(2,1)S(1)}, bf16[768,768]{1,0:T(8,128)(2,1)S(1)}, u32[]{:S(2)}, u32[]{:S(2)}) collective-permute-start(bf16[768,768]{1,0:T(8,128)(2,1)S(1)} %shard_map.17.first), channel_id=1, source_target_pairs={{0,192},{1,49},{2,194},{3,51},{4,196},{5,53},{6,198},{7,55},{8,200... | collective-permute-start | bytes 3538952 | tf_op jit(solution)/shard_map/ppermute | solution.py:187
  8.6 32.8 %collective-permute-start = (bf16[768,768]{1,0:T(8,128)(2,1)S(1)}, bf16[768,768]{1,0:T(8,128)(2,1)S(1)}, u32[]{:S(2)}, u32[]{:S(2)}) collective-permute-start(bf16[768,768]{1,0:T(8,128)(2,1)S(1)} %shard_map.17.first), channel_id=1, source_target_pairs={{0,16},{1,65},{2,18},{3,67},{4,20},{5,69},{6,22},{7,71},{8,24},{9,... | collective-permute-start | bytes 3538952 | tf_op jit(solution)/shard_map/ppermute | solution.py:188
  9.2 36.5 %collective-permute-start.2 = (bf16[256,768]{1,0:T(8,128)(2,1)S(1)}, bf16[256,768]{1,0:T(8,128)(2,1)S(1)}, u32[]{:S(2)}, u32[]{:S(2)}) collective-permute-start(bf16[256,768]{1,0:T(8,128)(2,1)S(1)} %shard_map.18.second), channel_id=1, source_target_pairs={{0,16},{1,65},{2,18},{3,67},{4,20},{5,69},{6,22},{7,71},{8,24},{9,... | collective-permute-start | bytes 1179656 | tf_op jit(solution)/shard_map/ppermute | solution.py:191
  11.6 34.0 %collective-permute-start.3 = (bf16[256,768]{1,0:T(8,128)(2,1)S(1)}, bf16[256,768]{1,0:T(8,128)(2,1)S(1)}, u32[]{:S(2)}, u32[]{:S(2)}) collective-permute-start(bf16[256,768]{1,0:T(8,128)(2,1)S(1)} %shard_map.18.second), channel_id=1, source_target_pairs={{0,192},{1,49},{2,194},{3,51},{4,196},{5,53},{6,198},{7,55},{8,200... | collective-permute-start | bytes 1179656 | tf_op jit(solution)/shard_map/ppermute | solution.py:190
  47.2 2.5 %collective-permute-start.4 = (f32[8,128]{1,0:T(8,128)S(1)}, f32[8,128]{1,0:T(8,128)S(1)}, u32[]{:S(2)}, u32[]{:S(2)}) collective-permute-start(f32[8,128]{1,0:T(8,128)S(1)} %get-tuple-element.23), channel_id=1, source_target_pairs={{16,0},{65,1},{18,2},{67,3},{20,4},{69,5},{22,6},{71,7},{24,8},{73... | collective-permute-start | bytes 12296 | tf_op jit(solution)/shard_map/ppermute | solution.py:208
  47.3 4.7 %collective-permute-start.5 = (f32[8,128]{1,0:T(8,128)S(1)}, f32[8,128]{1,0:T(8,128)S(1)}, u32[]{:S(2)}, u32[]{:S(2)}) collective-permute-start(f32[8,128]{1,0:T(8,128)S(1)} %get-tuple-element.24), channel_id=1, source_target_pairs={{192,0},{49,1},{194,2},{51,3},{196,4},{53,5},{198,6},{55,7},{200,8... | collective-permute-start | bytes 12296 | tf_op jit(solution)/shard_map/ppermute | solution.py:209

commit v9 on v8

--- a/solution.py
+++ b/solution.py
@@ -12,7 +12,6 @@
 LANES = 128
 STEP = 256
 FIRST = 768
-COPIES = 4
 
 sharpness = 10.0
 RATE = sharpness * math.log2(math.e)
@@ -85,22 +84,6 @@
         put(col_out, col_start, jnp.sum(total, axis=0, keepdims=True), col_add)
 
 
-def take_kernel(raw, taken, sems, *, start):
-    rows = taken.shape[0] // COPIES
-    copies = [
-        pltpu.make_async_copy(
-            raw.at[pl.ds(start + k * rows, rows), :],
-            taken.at[pl.ds(k * rows, rows), :],
-            sems.at[k],
-        )
-        for k in range(COPIES)
-    ]
-    for copy in copies:
-        copy.start()
-    for copy in copies:
-        copy.wait()
-
-
 def own_kernel(first, second, normed, density):
     unit_rows(first, normed.at[pl.ds(0, FIRST), :])
     unit_rows(second, normed.at[pl.ds(FIRST, second.shape[0]), :])
@@ -145,32 +128,20 @@
     keep[...] = weights[...] * rows / total
 
 
-def call(kernel, operands, outs, scratch=(), flops=0, space=pltpu.VMEM, limit=32):
+def call(kernel, operands, outs, scratch=(), flops=0):
     shapes = [jax.ShapeDtypeStruct(*out) for out in outs]
     moved = sum(math.prod(s.shape) * s.dtype.itemsize for s in [*operands, *shapes])
     return pl.pallas_call(
         kernel,
         out_shape=shapes,
-        in_specs=[pl.BlockSpec(memory_space=space)] * len(operands),
+        in_specs=[pl.BlockSpec(memory_space=pltpu.VMEM)] * len(operands),
         out_specs=[pl.BlockSpec(memory_space=pltpu.VMEM)] * len(shapes),
         scratch_shapes=list(scratch),
         cost_estimate=pl.CostEstimate(
             flops=flops, bytes_accessed=moved, transcendentals=0
         ),
-        compiler_params=pltpu.CompilerParams(vmem_limit_bytes=limit * 2**20),
+        compiler_params=pltpu.CompilerParams(vmem_limit_bytes=32 * 2**20),
     )(*operands)
-
-
-def take(rows, start, out):
-    (taken,) = call(
-        functools.partial(take_kernel, start=start),
-        [rows],
-        [out],
-        [pltpu.SemaphoreType.DMA((COPIES,))],
-        space=pltpu.HBM,
-        limit=16,
-    )
-    return taken
 
 
 def shards(embeddings):
@@ -183,10 +154,10 @@
     tile = 2 * rows * rows * width
     near_pairs, far_pairs = plan(players)
 
-    first = take(embeddings, 0, part)
+    first = embeddings[:FIRST]
     far_first = lax.ppermute(first, "dev", far_pairs)
     near_first = lax.ppermute(first, "dev", near_pairs)
-    second = take(embeddings, FIRST, rest)
+    second = embeddings[FIRST:]
     far_second = lax.ppermute(second, "dev", far_pairs)
     near_second = lax.ppermute(second, "dev", near_pairs)
     normed, density = call(own_kernel, [first, second], [block, sums], flops=tile)

time: 77.4 us -> 77.1 us (level)
  local copies, waits for them, and re-layouts: 1.41 us -> 2.37 us
  Pallas kernels: 8.32 us -> 7.5 us
    slice x0 -> x2, local copies, waits for them, and re-layouts: none -> 2.37 us  [the longest x1 1.35 us: shards(): first = embeddings[:FIRST]]
    unnamed x2 -> x0, local copies, waits for them, and re-layouts: 1.41 us -> none
    pallas_call x8 -> x6, Pallas kernels: 8.32 us -> 7.5 us  [call(): pl.pallas_call(kernel, out_shape=shapes, in_specs=[pl.BlockSpec(memory_sp...]
  transfers between devices with their start and end apart: 6 -> 6, of which waited for: 5 -> 5; matrix products, arithmetic and copies ran while one was open for 0% -> 1% of each run, Pallas kernels for 7% -> 7%
where the time goes in v9:
time: 77.1 us; the launch traced here: 76.9 us
  waiting for transfers between devices  31.4 us (41%)
  blocking collectives  24.5 us (32%)
  starting transfers between devices  11 us (14%)
  Pallas kernels  7.5 us (10%)
  local copies, waits for them, and re-layouts  2.37 us (3%)
    all_to_all x1, blocking collectives, shards(): totals = lax.all_to_all(total, 'dev', 0, 0, tiled=True)  24.5 us
    ppermute x1, waiting for transfers between devices, shards(): far_first = lax.ppermute(first, 'dev', far_pairs)  24.2 us
    pallas_call x6, Pallas kernels, call(): pl.pallas_call(kernel, out_shape=shapes, in_specs=[pl.BlockSpec(memory_sp...  7.5 us
    ppermute x1, starting transfers between devices, shards(): far_first = lax.ppermute(first, 'dev', far_pairs)  6.94 us
    ppermute x1, starting transfers between devices, shards(): near_second = lax.ppermute(second, 'dev', near_pairs)  2.46 us
    ppermute x1, waiting for transfers between devices, shards(): near_first = lax.ppermute(first, 'dev', near_pairs)  2.37 us
    ppermute x1, waiting for transfers between devices, shards(): from_far = lax.ppermute(to_far, 'dev', inverse(far_pairs))  2.21 us
    ppermute x1, waiting for transfers between devices, shards(): near_second = lax.ppermute(second, 'dev', near_pairs)  1.65 us
  transfers between devices with their start and end apart: 6, of which 5 were waited for; matrix products, arithmetic and copies ran while one was open for 1% of the time, Pallas kernels for 7%

profile of v9, /device:TPU:1, one launch (start us, length us, event | category | flops | bytes accessed | tf_op | source)
XLA Modules:
  0.0 76.9 jit_solution(16803493882448460546)
XLA Ops:
  0.0 1.3 %slice.6.first = bf16[768,768]{1,0:T(8,128)(2,1)S(1)} slice(bf16[1024,768]{1,0:T(8,128)(2,1)} %param.1), slice={[0:768], [0:768]} | slice | bytes 2359296 | tf_op jit(solution)/shard_map/slice | solution.py:157
  1.4 6.9 %collective-permute-start.1 = (bf16[768,768]{1,0:T(8,128)(2,1)S(1)}, bf16[768,768]{1,0:T(8,128)(2,1)S(1)}, u32[]{:S(2)}, u32[]{:S(2)}) collective-permute-start(bf16[768,768]{1,0:T(8,128)(2,1)S(1)} %slice.6.first), channel_id=1, source_target_pairs={{0,192},{1,49},{2,194},{3,51},{4,196},{5,53},{6,198},{7,55},{8,200... | collective-permute-start | bytes 3538952 | tf_op jit(solution)/shard_map/ppermute | solution.py:158
  8.3 0.0 collective-permute-start
  8.3 1.0 %slice.7.second = bf16[256,768]{1,0:T(8,128)(2,1)S(1)} slice(bf16[1024,768]{1,0:T(8,128)(2,1)} %param.1), slice={[768:1024], [0:768]} | slice | bytes 786432 | tf_op jit(solution)/shard_map/slice | solution.py:160
  9.3 2.5 %collective-permute-start.2 = (bf16[256,768]{1,0:T(8,128)(2,1)S(1)}, bf16[256,768]{1,0:T(8,128)(2,1)S(1)}, u32[]{:S(2)}, u32[]{:S(2)}) collective-permute-start(bf16[256,768]{1,0:T(8,128)(2,1)S(1)} %slice.7.second), channel_id=1, source_target_pairs={{0,16},{1,65},{2,18},{3,67},{4,20},{5,69},{6,22},{7,71},{8,24},{9,... | collective-permute-start | bytes 1179656 | tf_op jit(solution)/shard_map/ppermute | solution.py:162
  11.8 0.1 collective-permute-start.3
  11.9 2.3 %shard_map.17 = (bf16[1024,768]{1,0:T(8,128)(2,1)S(1)}, f32[8,128]{1,0:T(8,128)S(1)}) custom-call(bf16[768,768]{1,0:T(8,128)(2,1)S(1)} %slice.6.first, bf16[256,768]{1,0:T(8,128)(2,1)S(1)} %slice.7.second), custom_call_target="tpu_custom_call" | custom-call | flops 1610612736 | bytes 3149824 | tf_op jit(solution)/shard_map/pallas_call | solution.py:134
  14.2 24.2 %collective-permute-done.1.raw = bf16[768,768]{1,0:T(8,128)(2,1)S(1)} collective-permute-done((bf16[768,768]{1,0:T(8,128)(2,1)S(1)}, bf16[768,768]{1,0:T(8,128)(2,1)S(1)}, u32[]{:S(2)}, u32[]{:S(2)}) %collective-permute-start.1) | collective-permute-done | bytes 1179680 | tf_op jit(solution)/shard_map/ppermute | solution.py:158
  38.3 0.4 shard_map.18.far.far_first
  38.7 2.4 %collective-permute-done.near_raw = bf16[768,768]{1,0:T(8,128)(2,1)S(1)} collective-permute-done((bf16[768,768]{1,0:T(8,128)(2,1)S(1)}, bf16[768,768]{1,0:T(8,128)(2,1)S(1)}, u32[]{:S(2)}, u32[]{:S(2)}) %collective-permute-start) | collective-permute-done | bytes 1179680 | tf_op jit(solution)/shard_map/ppermute | solution.py:159
  41.1 2.6 %shard_map.19 = (f32[8,128]{1,0:T(8,128)S(1)}, bf16[768,768]{1,0:T(8,128)(2,1)S(1)}, f32[6,128]{1,0:T(8,128)S(1)}, f32[6,128]{1,0:T(8,128)S(1)}) custom-call(bf16[1024,768]{1,0:T(8,128)(2,1)S(1)} %get-tuple-element.16.normed, bf16[768,768]{1,0:T(8,128)(2,1)S(1)} %collective-permute-done.near_raw, bf16[768,768]{1,0:T(8,128)(2,1)S(1)} %shard_map.18.far.far_first, ...), custom_call_target="tpu_custom_call" | custom-call | flops 2113929216 | bytes 5126144 | tf_op jit(solution)/shard_map/pallas_call | solution.py:134
  43.7 1.7 %collective-permute-done.2.near_raw = bf16[256,768]{1,0:T(8,128)(2,1)S(1)} collective-permute-done((bf16[256,768]{1,0:T(8,128)(2,1)S(1)}, bf16[256,768]{1,0:T(8,128)(2,1)S(1)}, u32[]{:S(2)}, u32[]{:S(2)}) %collective-permute-start.2) | collective-permute-done | bytes 393248 | tf_op jit(solution)/shard_map/ppermute | solution.py:162
  45.3 0.0 collective-permute-done.3.far_raw
  45.3 1.5 %shard_map.20 = (f32[8,128]{1,0:T(8,128)S(1)}, f32[8,128]{1,0:T(8,128)S(1)}, f32[8,128]{1,0:T(8,128)S(1)}) custom-call(bf16[1024,768]{1,0:T(8,128)(2,1)S(1)} %get-tuple-element.16.normed, bf16[768,768]{1,0:T(8,128)(2,1)S(1)} %get-tuple-element.18.near_first, bf16[768,768]{1,0:T(8,128)(2,1)S(1)} %shard_map.18.far.far_first, ...), custom_call_target="tpu_custom_call" | custom-call | flops 1107296256 | bytes 4741120 | tf_op jit(solution)/shard_map/pallas_call | solution.py:134
  46.8 0.1 collective-permute-start.4
  46.9 1.4 %collective-permute-start.5 = (f32[8,128]{1,0:T(8,128)S(1)}, f32[8,128]{1,0:T(8,128)S(1)}, u32[]{:S(2)}, u32[]{:S(2)}) collective-permute-start(f32[8,128]{1,0:T(8,128)S(1)} %get-tuple-element.24), channel_id=1, source_target_pairs={{192,0},{49,1},{194,2},{51,3},{196,4},{53,5},{198,6},{55,7},{200,8... | collective-permute-start | bytes 12296 | tf_op jit(solution)/shard_map/ppermute | solution.py:180
  48.3 1.0 %collective-permute-done.4.from_near = f32[8,128]{1,0:T(8,128)S(1)} collective-permute-done((f32[8,128]{1,0:T(8,128)S(1)}, f32[8,128]{1,0:T(8,128)S(1)}, u32[]{:S(2)}, u32[]{:S(2)}) %collective-permute-start.4) | collective-permute-done | bytes 4128 | tf_op jit(solution)/shard_map/ppermute | solution.py:179
  49.4 2.2 %collective-permute-done.5.from_far = f32[8,128]{1,0:T(8,128)S(1)} collective-permute-done((f32[8,128]{1,0:T(8,128)S(1)}, f32[8,128]{1,0:T(8,128)S(1)}, u32[]{:S(2)}, u32[]{:S(2)}) %collective-permute-start.5) | collective-permute-done | bytes 4128 | tf_op jit(solution)/shard_map/ppermute | solution.py:180
  51.6 0.1 shard_map.21
  51.7 24.5 %all_to_all.11 = f32[256,1,128]{2,1,0:T(1,128)S(1)} all-to-all(f32[256,1,128]{2,1,0:T(1,128)S(1)} %bitcast.6), channel_id=1, replica_groups=mesh['dev'=256] {'dev'}, dimensions={0} | all-to-all | bytes 262144 | tf_op jit(solution)/shard_map/all_to_all | solution.py:184
  76.2 0.6 shard_map.22
Async XLA Ops:
  1.4 37.0 %collective-permute-start.1 = (bf16[768,768]{1,0:T(8,128)(2,1)S(1)}, bf16[768,768]{1,0:T(8,128)(2,1)S(1)}, u32[]{:S(2)}, u32[]{:S(2)}) collective-permute-start(bf16[768,768]{1,0:T(8,128)(2,1)S(1)} %slice.6.first), channel_id=1, source_target_pairs={{0,192},{1,49},{2,194},{3,51},{4,196},{5,53},{6,198},{7,55},{8,200... | collective-permute-start | bytes 3538952 | tf_op jit(solution)/shard_map/ppermute | solution.py:158
  8.3 32.8 %collective-permute-start = (bf16[768,768]{1,0:T(8,128)(2,1)S(1)}, bf16[768,768]{1,0:T(8,128)(2,1)S(1)}, u32[]{:S(2)}, u32[]{:S(2)}) collective-permute-start(bf16[768,768]{1,0:T(8,128)(2,1)S(1)} %slice.6.first), channel_id=1, source_target_pairs={{0,16},{1,65},{2,18},{3,67},{4,20},{5,69},{6,22},{7,71},{8,24},{9,... | collective-permute-start | bytes 3538952 | tf_op jit(solution)/shard_map/ppermute | solution.py:159
  9.3 36.0 %collective-permute-start.2 = (bf16[256,768]{1,0:T(8,128)(2,1)S(1)}, bf16[256,768]{1,0:T(8,128)(2,1)S(1)}, u32[]{:S(2)}, u32[]{:S(2)}) collective-permute-start(bf16[256,768]{1,0:T(8,128)(2,1)S(1)} %slice.7.second), channel_id=1, source_target_pairs={{0,16},{1,65},{2,18},{3,67},{4,20},{5,69},{6,22},{7,71},{8,24},{9,... | collective-permute-start | bytes 1179656 | tf_op jit(solution)/shard_map/ppermute | solution.py:162
  11.8 33.5 %collective-permute-start.3 = (bf16[256,768]{1,0:T(8,128)(2,1)S(1)}, bf16[256,768]{1,0:T(8,128)(2,1)S(1)}, u32[]{:S(2)}, u32[]{:S(2)}) collective-permute-start(bf16[256,768]{1,0:T(8,128)(2,1)S(1)} %slice.7.second), channel_id=1, source_target_pairs={{0,192},{1,49},{2,194},{3,51},{4,196},{5,53},{6,198},{7,55},{8,200... | collective-permute-start | bytes 1179656 | tf_op jit(solution)/shard_map/ppermute | solution.py:161
  46.8 2.5 %collective-permute-start.4 = (f32[8,128]{1,0:T(8,128)S(1)}, f32[8,128]{1,0:T(8,128)S(1)}, u32[]{:S(2)}, u32[]{:S(2)}) collective-permute-start(f32[8,128]{1,0:T(8,128)S(1)} %get-tuple-element.23), channel_id=1, source_target_pairs={{16,0},{65,1},{18,2},{67,3},{20,4},{69,5},{22,6},{71,7},{24,8},{73... | collective-permute-start | bytes 12296 | tf_op jit(solution)/shard_map/ppermute | solution.py:179
  46.9 4.7 %collective-permute-start.5 = (f32[8,128]{1,0:T(8,128)S(1)}, f32[8,128]{1,0:T(8,128)S(1)}, u32[]{:S(2)}, u32[]{:S(2)}) collective-permute-start(f32[8,128]{1,0:T(8,128)S(1)} %get-tuple-element.24), channel_id=1, source_target_pairs={{192,0},{49,1},{194,2},{51,3},{196,4},{53,5},{198,6},{55,7},{200,8... | collective-permute-start | bytes 12296 | tf_op jit(solution)/shard_map/ppermute | solution.py:180

commit v10 on v9

--- a/solution.py
+++ b/solution.py
@@ -3,6 +3,7 @@
 
 import jax
 import jax.numpy as jnp
+import numpy as np
 from jax import lax
 from jax.experimental import pallas as pl
 from jax.experimental.pallas import tpu as pltpu
@@ -181,7 +182,10 @@
     weights, total = call(
         weight_kernel, [density, from_near, from_far], [sums, ((players, LANES), f32)]
     )
-    totals = lax.all_to_all(total, "dev", 0, 0, tiled=True)
+    order = [int(peer) for peer in np.random.default_rng(1).permutation(players)]
+    totals = lax.all_to_all(
+        total, "dev", 0, 0, axis_index_groups=[order], tiled=True
+    )
     (keep,) = call(
         functools.partial(scale_kernel, rows=float(players * rows)), [weights, totals], [sums]
     )

time: 77.1 us -> 76.6 us (level)
  no operation moved by 1% of the time
where the time goes in v10:
time: 76.6 us; the launch traced here: 76.4 us
  waiting for transfers between devices  31.4 us (41%)
  blocking collectives  24.1 us (31%)
  starting transfers between devices  11 us (14%)
  Pallas kernels  7.5 us (10%)
  local copies, waits for them, and re-layouts  2.37 us (3%)
    ppermute x1, waiting for transfers between devices, shards(): far_first = lax.ppermute(first, 'dev', far_pairs)  24.2 us
    all_to_all x1, blocking collectives, shards(): lax.all_to_all(total, 'dev', 0, 0, axis_index_groups=[order], tiled=True)  24.1 us
    pallas_call x6, Pallas kernels, call(): pl.pallas_call(kernel, out_shape=shapes, in_specs=[pl.BlockSpec(memory_sp...  7.5 us
    ppermute x1, starting transfers between devices, shards(): far_first = lax.ppermute(first, 'dev', far_pairs)  6.94 us
    ppermute x1, starting transfers between devices, shards(): near_second = lax.ppermute(second, 'dev', near_pairs)  2.46 us
    ppermute x1, waiting for transfers between devices, shards(): near_first = lax.ppermute(first, 'dev', near_pairs)  2.37 us
    ppermute x1, waiting for transfers between devices, shards(): from_far = lax.ppermute(to_far, 'dev', inverse(far_pairs))  2.21 us
    ppermute x1, waiting for transfers between devices, shards(): near_second = lax.ppermute(second, 'dev', near_pairs)  1.65 us
  transfers between devices with their start and end apart: 6, of which 5 were waited for; matrix products, arithmetic and copies ran while one was open for 1% of the time, Pallas kernels for 7%

profile of v10, /device:TPU:1, one launch (start us, length us, event | category | flops | bytes accessed | tf_op | source)
XLA Modules:
  0.0 76.4 jit_solution(5482460654045672532)
XLA Ops:
  0.0 1.3 %slice.6.first = bf16[768,768]{1,0:T(8,128)(2,1)S(1)} slice(bf16[1024,768]{1,0:T(8,128)(2,1)} %param.1), slice={[0:768], [0:768]} | slice | bytes 2359296 | tf_op jit(solution)/shard_map/slice | solution.py:158
  1.4 6.9 %collective-permute-start.1 = (bf16[768,768]{1,0:T(8,128)(2,1)S(1)}, bf16[768,768]{1,0:T(8,128)(2,1)S(1)}, u32[]{:S(2)}, u32[]{:S(2)}) collective-permute-start(bf16[768,768]{1,0:T(8,128)(2,1)S(1)} %slice.6.first), channel_id=1, source_target_pairs={{0,192},{1,49},{2,194},{3,51},{4,196},{5,53},{6,198},{7,55},{8,200... | collective-permute-start | bytes 3538952 | tf_op jit(solution)/shard_map/ppermute | solution.py:159
  8.3 0.0 collective-permute-start
  8.3 1.0 %slice.7.second = bf16[256,768]{1,0:T(8,128)(2,1)S(1)} slice(bf16[1024,768]{1,0:T(8,128)(2,1)} %param.1), slice={[768:1024], [0:768]} | slice | bytes 786432 | tf_op jit(solution)/shard_map/slice | solution.py:161
  9.3 2.5 %collective-permute-start.2 = (bf16[256,768]{1,0:T(8,128)(2,1)S(1)}, bf16[256,768]{1,0:T(8,128)(2,1)S(1)}, u32[]{:S(2)}, u32[]{:S(2)}) collective-permute-start(bf16[256,768]{1,0:T(8,128)(2,1)S(1)} %slice.7.second), channel_id=1, source_target_pairs={{0,16},{1,65},{2,18},{3,67},{4,20},{5,69},{6,22},{7,71},{8,24},{9,... | collective-permute-start | bytes 1179656 | tf_op jit(solution)/shard_map/ppermute | solution.py:163
  11.8 0.1 collective-permute-start.3
  11.9 2.3 %shard_map.17 = (bf16[1024,768]{1,0:T(8,128)(2,1)S(1)}, f32[8,128]{1,0:T(8,128)S(1)}) custom-call(bf16[768,768]{1,0:T(8,128)(2,1)S(1)} %slice.6.first, bf16[256,768]{1,0:T(8,128)(2,1)S(1)} %slice.7.second), custom_call_target="tpu_custom_call" | custom-call | flops 1610612736 | bytes 3149824 | tf_op jit(solution)/shard_map/pallas_call | solution.py:135
  14.2 24.2 %collective-permute-done.1.raw = bf16[768,768]{1,0:T(8,128)(2,1)S(1)} collective-permute-done((bf16[768,768]{1,0:T(8,128)(2,1)S(1)}, bf16[768,768]{1,0:T(8,128)(2,1)S(1)}, u32[]{:S(2)}, u32[]{:S(2)}) %collective-permute-start.1) | collective-permute-done | bytes 1179680 | tf_op jit(solution)/shard_map/ppermute | solution.py:159
  38.3 0.4 shard_map.18.far.far_first
  38.7 2.4 %collective-permute-done.near_raw = bf16[768,768]{1,0:T(8,128)(2,1)S(1)} collective-permute-done((bf16[768,768]{1,0:T(8,128)(2,1)S(1)}, bf16[768,768]{1,0:T(8,128)(2,1)S(1)}, u32[]{:S(2)}, u32[]{:S(2)}) %collective-permute-start) | collective-permute-done | bytes 1179680 | tf_op jit(solution)/shard_map/ppermute | solution.py:160
  41.1 2.6 %shard_map.19 = (f32[8,128]{1,0:T(8,128)S(1)}, bf16[768,768]{1,0:T(8,128)(2,1)S(1)}, f32[6,128]{1,0:T(8,128)S(1)}, f32[6,128]{1,0:T(8,128)S(1)}) custom-call(bf16[1024,768]{1,0:T(8,128)(2,1)S(1)} %get-tuple-element.16.normed, bf16[768,768]{1,0:T(8,128)(2,1)S(1)} %collective-permute-done.near_raw, bf16[768,768]{1,0:T(8,128)(2,1)S(1)} %shard_map.18.far.far_first, ...), custom_call_target="tpu_custom_call" | custom-call | flops 2113929216 | bytes 5126144 | tf_op jit(solution)/shard_map/pallas_call | solution.py:135
  43.7 1.7 %collective-permute-done.2.near_raw = bf16[256,768]{1,0:T(8,128)(2,1)S(1)} collective-permute-done((bf16[256,768]{1,0:T(8,128)(2,1)S(1)}, bf16[256,768]{1,0:T(8,128)(2,1)S(1)}, u32[]{:S(2)}, u32[]{:S(2)}) %collective-permute-start.2) | collective-permute-done | bytes 393248 | tf_op jit(solution)/shard_map/ppermute | solution.py:163
  45.3 0.0 collective-permute-done.3.far_raw
  45.3 1.5 %shard_map.20 = (f32[8,128]{1,0:T(8,128)S(1)}, f32[8,128]{1,0:T(8,128)S(1)}, f32[8,128]{1,0:T(8,128)S(1)}) custom-call(bf16[1024,768]{1,0:T(8,128)(2,1)S(1)} %get-tuple-element.16.normed, bf16[768,768]{1,0:T(8,128)(2,1)S(1)} %get-tuple-element.18.near_first, bf16[768,768]{1,0:T(8,128)(2,1)S(1)} %shard_map.18.far.far_first, ...), custom_call_target="tpu_custom_call" | custom-call | flops 1107296256 | bytes 4741120 | tf_op jit(solution)/shard_map/pallas_call | solution.py:135
  46.8 0.1 collective-permute-start.4
  46.9 1.4 %collective-permute-start.5 = (f32[8,128]{1,0:T(8,128)S(1)}, f32[8,128]{1,0:T(8,128)S(1)}, u32[]{:S(2)}, u32[]{:S(2)}) collective-permute-start(f32[8,128]{1,0:T(8,128)S(1)} %get-tuple-element.24), channel_id=1, source_target_pairs={{192,0},{49,1},{194,2},{51,3},{196,4},{53,5},{198,6},{55,7},{200,8... | collective-permute-start | bytes 12296 | tf_op jit(solution)/shard_map/ppermute | solution.py:181
  48.3 1.0 %collective-permute-done.4.from_near = f32[8,128]{1,0:T(8,128)S(1)} collective-permute-done((f32[8,128]{1,0:T(8,128)S(1)}, f32[8,128]{1,0:T(8,128)S(1)}, u32[]{:S(2)}, u32[]{:S(2)}) %collective-permute-start.4) | collective-permute-done | bytes 4128 | tf_op jit(solution)/shard_map/ppermute | solution.py:180
  49.4 2.2 %collective-permute-done.5.from_far = f32[8,128]{1,0:T(8,128)S(1)} collective-permute-done((f32[8,128]{1,0:T(8,128)S(1)}, f32[8,128]{1,0:T(8,128)S(1)}, u32[]{:S(2)}, u32[]{:S(2)}) %collective-permute-start.5) | collective-permute-done | bytes 4128 | tf_op jit(solution)/shard_map/ppermute | solution.py:181
  51.6 0.1 shard_map.21
  51.7 24.1 %all_to_all.11 = f32[256,1,128]{2,1,0:T(1,128)S(1)} all-to-all(f32[256,1,128]{2,1,0:T(1,128)S(1)} %bitcast.6), channel_id=1, replica_groups={{29,138,13,78,155,120,204,7,183,153,167,124,80,43,99,21,156,127,150,86,..., dimensions={0} | all-to-all | bytes 262144 | tf_op jit(solution)/shard_map/all_to_all | solution.py:186
  75.8 0.6 shard_map.22
Async XLA Ops:
  1.4 37.0 %collective-permute-start.1 = (bf16[768,768]{1,0:T(8,128)(2,1)S(1)}, bf16[768,768]{1,0:T(8,128)(2,1)S(1)}, u32[]{:S(2)}, u32[]{:S(2)}) collective-permute-start(bf16[768,768]{1,0:T(8,128)(2,1)S(1)} %slice.6.first), channel_id=1, source_target_pairs={{0,192},{1,49},{2,194},{3,51},{4,196},{5,53},{6,198},{7,55},{8,200... | collective-permute-start | bytes 3538952 | tf_op jit(solution)/shard_map/ppermute | solution.py:159
  8.3 32.8 %collective-permute-start = (bf16[768,768]{1,0:T(8,128)(2,1)S(1)}, bf16[768,768]{1,0:T(8,128)(2,1)S(1)}, u32[]{:S(2)}, u32[]{:S(2)}) collective-permute-start(bf16[768,768]{1,0:T(8,128)(2,1)S(1)} %slice.6.first), channel_id=1, source_target_pairs={{0,16},{1,65},{2,18},{3,67},{4,20},{5,69},{6,22},{7,71},{8,24},{9,... | collective-permute-start | bytes 3538952 | tf_op jit(solution)/shard_map/ppermute | solution.py:160
  9.3 36.0 %collective-permute-start.2 = (bf16[256,768]{1,0:T(8,128)(2,1)S(1)}, bf16[256,768]{1,0:T(8,128)(2,1)S(1)}, u32[]{:S(2)}, u32[]{:S(2)}) collective-permute-start(bf16[256,768]{1,0:T(8,128)(2,1)S(1)} %slice.7.second), channel_id=1, source_target_pairs={{0,16},{1,65},{2,18},{3,67},{4,20},{5,69},{6,22},{7,71},{8,24},{9,... | collective-permute-start | bytes 1179656 | tf_op jit(solution)/shard_map/ppermute | solution.py:163
  11.8 33.5 %collective-permute-start.3 = (bf16[256,768]{1,0:T(8,128)(2,1)S(1)}, bf16[256,768]{1,0:T(8,128)(2,1)S(1)}, u32[]{:S(2)}, u32[]{:S(2)}) collective-permute-start(bf16[256,768]{1,0:T(8,128)(2,1)S(1)} %slice.7.second), channel_id=1, source_target_pairs={{0,192},{1,49},{2,194},{3,51},{4,196},{5,53},{6,198},{7,55},{8,200... | collective-permute-start | bytes 1179656 | tf_op jit(solution)/shard_map/ppermute | solution.py:162
  46.8 2.5 %collective-permute-start.4 = (f32[8,128]{1,0:T(8,128)S(1)}, f32[8,128]{1,0:T(8,128)S(1)}, u32[]{:S(2)}, u32[]{:S(2)}) collective-permute-start(f32[8,128]{1,0:T(8,128)S(1)} %get-tuple-element.23), channel_id=1, source_target_pairs={{16,0},{65,1},{18,2},{67,3},{20,4},{69,5},{22,6},{71,7},{24,8},{73... | collective-permute-start | bytes 12296 | tf_op jit(solution)/shard_map/ppermute | solution.py:180
  46.9 4.7 %collective-permute-start.5 = (f32[8,128]{1,0:T(8,128)S(1)}, f32[8,128]{1,0:T(8,128)S(1)}, u32[]{:S(2)}, u32[]{:S(2)}) collective-permute-start(f32[8,128]{1,0:T(8,128)S(1)} %get-tuple-element.24), channel_id=1, source_target_pairs={{192,0},{49,1},{194,2},{51,3},{196,4},{53,5},{198,6},{55,7},{200,8... | collective-permute-start | bytes 12296 | tf_op jit(solution)/shard_map/ppermute | solution.py:181

commit v11 on v10

--- a/solution.py
+++ b/solution.py
@@ -125,7 +125,7 @@
 
 
 def scale_kernel(weights, totals, keep, *, rows):
-    total = jnp.sum(totals[...], axis=0, keepdims=True)
+    total = jnp.sum(totals[...], axis=0, keepdims=True)[:, :1]
     keep[...] = weights[...] * rows / total
 
 
@@ -180,7 +180,7 @@
     from_near = lax.ppermute(to_near, "dev", inverse(near_pairs))
     from_far = lax.ppermute(to_far, "dev", inverse(far_pairs))
     weights, total = call(
-        weight_kernel, [density, from_near, from_far], [sums, ((players, LANES), f32)]
+        weight_kernel, [density, from_near, from_far], [sums, ((players, 8), f32)]
     )
     order = [int(peer) for peer in np.random.default_rng(1).permutation(players)]
     totals = lax.all_to_all(

time: 76.6 us -> 76.7 us (level)
  no operation moved by 1% of the time
where the time goes in v11:
time: 76.7 us; the launch traced here: 76.5 us
  waiting for transfers between devices  31.4 us (41%)
  blocking collectives  24.1 us (31%)
  starting transfers between devices  11 us (14%)
  Pallas kernels  7.57 us (10%)
  local copies, waits for them, and re-layouts  2.37 us (3%)
    ppermute x1, waiting for transfers between devices, shards(): far_first = lax.ppermute(first, 'dev', far_pairs)  24.2 us
    all_to_all x1, blocking collectives, shards(): lax.all_to_all(total, 'dev', 0, 0, axis_index_groups=[order], tiled=True)  24.1 us
    pallas_call x6, Pallas kernels, call(): pl.pallas_call(kernel, out_shape=shapes, in_specs=[pl.BlockSpec(memory_sp...  7.57 us
    ppermute x1, starting transfers between devices, shards(): far_first = lax.ppermute(first, 'dev', far_pairs)  6.94 us
    ppermute x1, starting transfers between devices, shards(): near_second = lax.ppermute(second, 'dev', near_pairs)  2.46 us
    ppermute x1, waiting for transfers between devices, shards(): near_first = lax.ppermute(first, 'dev', near_pairs)  2.37 us
    ppermute x1, waiting for transfers between devices, shards(): from_far = lax.ppermute(to_far, 'dev', inverse(far_pairs))  2.21 us
    ppermute x1, waiting for transfers between devices, shards(): near_second = lax.ppermute(second, 'dev', near_pairs)  1.65 us
  transfers between devices with their start and end apart: 6, of which 5 were waited for; matrix products, arithmetic and copies ran while one was open for 1% of the time, Pallas kernels for 7%

profile of v11, /device:TPU:1, one launch (start us, length us, event | category | flops | bytes accessed | tf_op | source)
XLA Modules:
  0.0 76.5 jit_solution(13194733920756947792)
XLA Ops:
  0.0 1.3 %slice.6.first = bf16[768,768]{1,0:T(8,128)(2,1)S(1)} slice(bf16[1024,768]{1,0:T(8,128)(2,1)} %param.1), slice={[0:768], [0:768]} | slice | bytes 2359296 | tf_op jit(solution)/shard_map/slice | solution.py:158
  1.4 6.9 %collective-permute-start.1 = (bf16[768,768]{1,0:T(8,128)(2,1)S(1)}, bf16[768,768]{1,0:T(8,128)(2,1)S(1)}, u32[]{:S(2)}, u32[]{:S(2)}) collective-permute-start(bf16[768,768]{1,0:T(8,128)(2,1)S(1)} %slice.6.first), channel_id=1, source_target_pairs={{0,192},{1,49},{2,194},{3,51},{4,196},{5,53},{6,198},{7,55},{8,200... | collective-permute-start | bytes 3538952 | tf_op jit(solution)/shard_map/ppermute | solution.py:159
  8.3 0.0 collective-permute-start
  8.3 1.0 %slice.7.second = bf16[256,768]{1,0:T(8,128)(2,1)S(1)} slice(bf16[1024,768]{1,0:T(8,128)(2,1)} %param.1), slice={[768:1024], [0:768]} | slice | bytes 786432 | tf_op jit(solution)/shard_map/slice | solution.py:161
  9.3 2.5 %collective-permute-start.2 = (bf16[256,768]{1,0:T(8,128)(2,1)S(1)}, bf16[256,768]{1,0:T(8,128)(2,1)S(1)}, u32[]{:S(2)}, u32[]{:S(2)}) collective-permute-start(bf16[256,768]{1,0:T(8,128)(2,1)S(1)} %slice.7.second), channel_id=1, source_target_pairs={{0,16},{1,65},{2,18},{3,67},{4,20},{5,69},{6,22},{7,71},{8,24},{9,... | collective-permute-start | bytes 1179656 | tf_op jit(solution)/shard_map/ppermute | solution.py:163
  11.8 0.1 collective-permute-start.3
  11.9 2.3 %shard_map.17 = (bf16[1024,768]{1,0:T(8,128)(2,1)S(1)}, f32[8,128]{1,0:T(8,128)S(1)}) custom-call(bf16[768,768]{1,0:T(8,128)(2,1)S(1)} %slice.6.first, bf16[256,768]{1,0:T(8,128)(2,1)S(1)} %slice.7.second), custom_call_target="tpu_custom_call" | custom-call | flops 1610612736 | bytes 3149824 | tf_op jit(solution)/shard_map/pallas_call | solution.py:135
  14.2 24.2 %collective-permute-done.1.raw = bf16[768,768]{1,0:T(8,128)(2,1)S(1)} collective-permute-done((bf16[768,768]{1,0:T(8,128)(2,1)S(1)}, bf16[768,768]{1,0:T(8,128)(2,1)S(1)}, u32[]{:S(2)}, u32[]{:S(2)}) %collective-permute-start.1) | collective-permute-done | bytes 1179680 | tf_op jit(solution)/shard_map/ppermute | solution.py:159
  38.3 0.4 shard_map.18.far.far_first
  38.7 2.4 %collective-permute-done.near_raw = bf16[768,768]{1,0:T(8,128)(2,1)S(1)} collective-permute-done((bf16[768,768]{1,0:T(8,128)(2,1)S(1)}, bf16[768,768]{1,0:T(8,128)(2,1)S(1)}, u32[]{:S(2)}, u32[]{:S(2)}) %collective-permute-start) | collective-permute-done | bytes 1179680 | tf_op jit(solution)/shard_map/ppermute | solution.py:160
  41.1 2.6 %shard_map.19 = (f32[8,128]{1,0:T(8,128)S(1)}, bf16[768,768]{1,0:T(8,128)(2,1)S(1)}, f32[6,128]{1,0:T(8,128)S(1)}, f32[6,128]{1,0:T(8,128)S(1)}) custom-call(bf16[1024,768]{1,0:T(8,128)(2,1)S(1)} %get-tuple-element.16.normed, bf16[768,768]{1,0:T(8,128)(2,1)S(1)} %collective-permute-done.near_raw, bf16[768,768]{1,0:T(8,128)(2,1)S(1)} %shard_map.18.far.far_first, ...), custom_call_target="tpu_custom_call" | custom-call | flops 2113929216 | bytes 5126144 | tf_op jit(solution)/shard_map/pallas_call | solution.py:135
  43.7 1.7 %collective-permute-done.2.near_raw = bf16[256,768]{1,0:T(8,128)(2,1)S(1)} collective-permute-done((bf16[256,768]{1,0:T(8,128)(2,1)S(1)}, bf16[256,768]{1,0:T(8,128)(2,1)S(1)}, u32[]{:S(2)}, u32[]{:S(2)}) %collective-permute-start.2) | collective-permute-done | bytes 393248 | tf_op jit(solution)/shard_map/ppermute | solution.py:163
  45.3 0.0 collective-permute-done.3.far_raw
  45.3 1.5 %shard_map.20 = (f32[8,128]{1,0:T(8,128)S(1)}, f32[8,128]{1,0:T(8,128)S(1)}, f32[8,128]{1,0:T(8,128)S(1)}) custom-call(bf16[1024,768]{1,0:T(8,128)(2,1)S(1)} %get-tuple-element.16.normed, bf16[768,768]{1,0:T(8,128)(2,1)S(1)} %get-tuple-element.18.near_first, bf16[768,768]{1,0:T(8,128)(2,1)S(1)} %shard_map.18.far.far_first, ...), custom_call_target="tpu_custom_call" | custom-call | flops 1107296256 | bytes 4741120 | tf_op jit(solution)/shard_map/pallas_call | solution.py:135
  46.8 0.1 collective-permute-start.4
  46.9 1.4 %collective-permute-start.5 = (f32[8,128]{1,0:T(8,128)S(1)}, f32[8,128]{1,0:T(8,128)S(1)}, u32[]{:S(2)}, u32[]{:S(2)}) collective-permute-start(f32[8,128]{1,0:T(8,128)S(1)} %get-tuple-element.24), channel_id=1, source_target_pairs={{192,0},{49,1},{194,2},{51,3},{196,4},{53,5},{198,6},{55,7},{200,8... | collective-permute-start | bytes 12296 | tf_op jit(solution)/shard_map/ppermute | solution.py:181
  48.3 1.0 %collective-permute-done.4.from_near = f32[8,128]{1,0:T(8,128)S(1)} collective-permute-done((f32[8,128]{1,0:T(8,128)S(1)}, f32[8,128]{1,0:T(8,128)S(1)}, u32[]{:S(2)}, u32[]{:S(2)}) %collective-permute-start.4) | collective-permute-done | bytes 4128 | tf_op jit(solution)/shard_map/ppermute | solution.py:180
  49.4 2.2 %collective-permute-done.5.from_far = f32[8,128]{1,0:T(8,128)S(1)} collective-permute-done((f32[8,128]{1,0:T(8,128)S(1)}, f32[8,128]{1,0:T(8,128)S(1)}, u32[]{:S(2)}, u32[]{:S(2)}) %collective-permute-start.5) | collective-permute-done | bytes 4128 | tf_op jit(solution)/shard_map/ppermute | solution.py:181
  51.6 0.1 shard_map.21
  51.7 24.1 %all_to_all.11 = f32[256,1,8]{2,1,0:T(1,128)S(1)} all-to-all(f32[256,1,8]{2,1,0:T(1,128)S(1)} %bitcast.6), channel_id=1, replica_groups={{29,138,13,78,155,120,204,7,183,153,167,124,80,43,99,21,156,127,150,86,..., dimensions={0} | all-to-all | bytes 16384 | tf_op jit(solution)/shard_map/all_to_all | solution.py:186
  75.8 0.7 shard_map.22
Async XLA Ops:
  1.4 37.0 %collective-permute-start.1 = (bf16[768,768]{1,0:T(8,128)(2,1)S(1)}, bf16[768,768]{1,0:T(8,128)(2,1)S(1)}, u32[]{:S(2)}, u32[]{:S(2)}) collective-permute-start(bf16[768,768]{1,0:T(8,128)(2,1)S(1)} %slice.6.first), channel_id=1, source_target_pairs={{0,192},{1,49},{2,194},{3,51},{4,196},{5,53},{6,198},{7,55},{8,200... | collective-permute-start | bytes 3538952 | tf_op jit(solution)/shard_map/ppermute | solution.py:159
  8.3 32.8 %collective-permute-start = (bf16[768,768]{1,0:T(8,128)(2,1)S(1)}, bf16[768,768]{1,0:T(8,128)(2,1)S(1)}, u32[]{:S(2)}, u32[]{:S(2)}) collective-permute-start(bf16[768,768]{1,0:T(8,128)(2,1)S(1)} %slice.6.first), channel_id=1, source_target_pairs={{0,16},{1,65},{2,18},{3,67},{4,20},{5,69},{6,22},{7,71},{8,24},{9,... | collective-permute-start | bytes 3538952 | tf_op jit(solution)/shard_map/ppermute | solution.py:160
  9.3 36.0 %collective-permute-start.2 = (bf16[256,768]{1,0:T(8,128)(2,1)S(1)}, bf16[256,768]{1,0:T(8,128)(2,1)S(1)}, u32[]{:S(2)}, u32[]{:S(2)}) collective-permute-start(bf16[256,768]{1,0:T(8,128)(2,1)S(1)} %slice.7.second), channel_id=1, source_target_pairs={{0,16},{1,65},{2,18},{3,67},{4,20},{5,69},{6,22},{7,71},{8,24},{9,... | collective-permute-start | bytes 1179656 | tf_op jit(solution)/shard_map/ppermute | solution.py:163
  11.8 33.5 %collective-permute-start.3 = (bf16[256,768]{1,0:T(8,128)(2,1)S(1)}, bf16[256,768]{1,0:T(8,128)(2,1)S(1)}, u32[]{:S(2)}, u32[]{:S(2)}) collective-permute-start(bf16[256,768]{1,0:T(8,128)(2,1)S(1)} %slice.7.second), channel_id=1, source_target_pairs={{0,192},{1,49},{2,194},{3,51},{4,196},{5,53},{6,198},{7,55},{8,200... | collective-permute-start | bytes 1179656 | tf_op jit(solution)/shard_map/ppermute | solution.py:162
  46.8 2.5 %collective-permute-start.4 = (f32[8,128]{1,0:T(8,128)S(1)}, f32[8,128]{1,0:T(8,128)S(1)}, u32[]{:S(2)}, u32[]{:S(2)}) collective-permute-start(f32[8,128]{1,0:T(8,128)S(1)} %get-tuple-element.23), channel_id=1, source_target_pairs={{16,0},{65,1},{18,2},{67,3},{20,4},{69,5},{22,6},{71,7},{24,8},{73... | collective-permute-start | bytes 12296 | tf_op jit(solution)/shard_map/ppermute | solution.py:180
  46.9 4.7 %collective-permute-start.5 = (f32[8,128]{1,0:T(8,128)S(1)}, f32[8,128]{1,0:T(8,128)S(1)}, u32[]{:S(2)}, u32[]{:S(2)}) collective-permute-start(f32[8,128]{1,0:T(8,128)S(1)} %get-tuple-element.24), channel_id=1, source_target_pairs={{192,0},{49,1},{194,2},{51,3},{196,4},{53,5},{198,6},{55,7},{200,8... | collective-permute-start | bytes 12296 | tf_op jit(solution)/shard_map/ppermute | solution.py:181
